TPU v7x, 256 devices: a whole 4x4x8 slice. The times are simulated.
256 devices in a mesh: row: 32 (over y, x, core), col: 8 (over z).
Axes of the slice: x: 4, y: 4, z: 8, core: 2. Of those that a mesh axis runs over, the one named last changes fastest.
Arguments:
- adjoint: float32 [4, 4, 4096, 1024], P(None, None, 'row', 'col'), may hold values from -24 to 24
- rate_scale: float32 [4, 4, 4096, 1024], P(None, None, 'row', 'col'), may hold values from 0.5 to 2
- kinetics: float32 [4, 4], replicated, may hold values from -3 to 3
- cross_matrix: float32 [4, 4], replicated, may hold values from -3 to 3
- x_diffusion: float32 [4, 4096], replicated, may hold values from 1 to 64
- y_diffusion: float32 [4, 1024], replicated, may hold values from 1 to 64
Outputs:
- adjoint_out: float32 [4, 4, 4096, 1024], P(None, None, 'row', 'col')
All inputs are finite; a program needn't handle non-finite values.
Results may differ from a plain program's by a relative error of at most 0.0004.
Values sent between devices are 32-bit elements; how exact they have to be, the bound alone decides.
No kernel may reach another device: no remote copies, remote signals or barrier semaphores. Data moves between devices by JAX's collectives and lax.ppermute only.
A program may use at most 192 MiB of HBM per device.

v0:
```python
import functools

import jax
import jax.numpy as jnp
from jax import lax
from jax.experimental import pallas as pl
from jax.experimental.pallas import tpu as pltpu
from jax.sharding import PartitionSpec as P

STEPS = 2
M = 1000.0
N = 128
EXT = N + 8
f32 = jnp.float32
bf16 = jnp.bfloat16
VMEM = 56 * 1024 * 1024


def iota(shape, dim):
    return lax.broadcasted_iota(jnp.int32, shape, dim)


def split(a):
    hi = a.astype(bf16)
    return hi, (a - hi.astype(f32)).astype(bf16)


def dot3(a, b, nt=False):
    dims = (((1,), (1 if nt else 0,)), ((), ()))
    ah, al = split(a)
    bh, bl = split(b)

    def dot(p, q):
        return lax.dot_general(p, q, dims, preferred_element_type=f32)

    return dot(ah, bh) + (dot(ah, bl) + dot(al, bh))


def tables_kernel(
    nx, ny, xd, yd, gx, lx, hx, gy, ry, hy, wx, wy,
    rows_x, rows_y, ex, ey, p0, p1, q0, q1,
):
    k = lax.axis_index("row")
    l = lax.axis_index("col")
    scale = 1.0 / M
    rows_x[...] = jnp.full((N, N), scale, f32)
    rows_y[...] = jnp.full((N, N), scale, f32)
    for j in range(nx):
        rows_x[4 * j : 4 * j + 4, :] = scale / xd[:, j * N : (j + 1) * N]
    for j in range(ny):
        rows_y[4 * j : 4 * j + 4, :] = scale / yd[:, j * N : (j + 1) * N]

    def block(ref, index):
        return scale / ref[:, pl.ds(pl.multiple_of(index * N, N), N)]

    rows_y[32:36, :] = block(xd, k)
    rows_y[36:40, :] = block(yd, l)
    rows_y[40:44, :] = block(xd, jnp.maximum(k - 1, 0)) * (k > 0).astype(f32)
    rows_y[44:48, :] = block(yd, jnp.maximum(l - 1, 0)) * (l > 0).astype(f32)
    rows_y[48:52, :] = block(xd, jnp.minimum(k + 1, nx - 1)) * (k < nx - 1).astype(f32)
    rows_y[52:56, :] = block(yd, jnp.minimum(l + 1, ny - 1)) * (l < ny - 1).astype(f32)
    ex[...] = rows_x[...].T
    ey[...] = rows_y[...].T

    first2 = (iota((2, N), 0) == 0).astype(f32)
    one, zero = jnp.ones((1, N), f32), jnp.zeros((1, N), f32)

    def body(i, carry):
        vx, dx, va, da, vb, db, ux, cx, ua, ca, ub, cb = carry
        at = pl.multiple_of(i * 8, 8)
        back = pl.multiple_of(N - 8 - i * 8, 8)
        ex_f, ey_f = ex[pl.ds(at, 8), :], ey[pl.ds(at, 8), :]
        ex_b, ey_b = ex[pl.ds(back, 8), :], ey[pl.ds(back, 8), :]
        for r in range(8):
            t = at + r
            p0[pl.ds(t, 1), :] = va
            p1[pl.ds(t, 1), :] = vb
            e, ee = ex_f[r : r + 1], ey_f[r : r + 1]
            dx = dx + e * vx
            vx = vx + dx
            da = da + ee * va
            va = va + da
            db = db + ee * vb
            vb = vb + db
            r2 = 7 - r
            t = back + r2
            q0[pl.ds(t, 1), :] = ua
            q1[pl.ds(t, 1), :] = ub
            e, ee = ex_b[r2 : r2 + 1], ey_b[r2 : r2 + 1]
            cx = cx + e * ux
            ux = ux + cx
            ca = ca + ee * ua
            ua = ua + ca
            cb = cb + ee * ub
            ub = ub + cb
        return vx, dx, va, da, vb, db, ux, cx, ua, ca, ub, cb

    init = (first2, 1.0 - first2, one, zero, zero, one)
    vx, dx, va, da, vb, db, ux, cx, ua, ca, ub, cb = lax.fori_loop(
        0, N // 8, body, init + init
    )

    row = iota((8, N), 0)
    lane = iota((8, N), 1)
    blk = lane // 4
    forward = row < 2
    is_x = row % 2 == 0
    count = jnp.where(is_x, nx, ny)
    own = jnp.where(is_x, k, l)
    place = jnp.where(forward, blk, count - 1 - blk)
    own = jnp.where(forward, own, count - 1 - own)

    def pack(a, b, c, d):
        return jnp.where(
            row == 0, a, jnp.where(row == 1, b, jnp.where(row == 2, c, d))
        )

    def shifted(a, by):
        return jnp.where(
            forward, pltpu.roll(a, 4 * by, 1), pltpu.roll(a, N - 4 * by, 1)
        )

    def outside(by):
        return place < by

    a0 = pack(vx[0:1], va, ux[0:1], ua)
    b0 = pack(vx[1:2], vb, ux[1:2], ub)
    c0 = pack(dx[0:1], da, cx[0:1], ca)
    d0 = pack(dx[1:2], db, cx[1:2], cb)
    a, b, c, d = a0, b0, c0, d0
    by = 1
    while by < max(nx, ny):
        skip = outside(by)
        sa = jnp.where(skip, 1.0, shifted(a, by))
        sb = jnp.where(skip, 0.0, shifted(b, by))
        sc = jnp.where(skip, 0.0, shifted(c, by))
        sd = jnp.where(skip, 1.0, shifted(d, by))
        a, b, c, d = a * sa + b * sc, a * sb + b * sd, c * sa + d * sc, c * sb + d * sd
        norm = 1.0 / (a + b)
        a, b, c, d = a * norm, b * norm, c * norm, d * norm
        by *= 2
    skip = outside(1)
    slope = jnp.where(skip, 1.0, shifted((c + d) / (a + b), 1))

    decay = (1.0 - slope) / ((a0 + b0 * slope) - (c0 + d0 * slope))
    between = (place < own) & (place >= 0)
    prod = jnp.where(between, decay, 1.0)

    def against(a, by):
        return jnp.where(
            forward, pltpu.roll(a, N - 4 * by, 1), pltpu.roll(a, 4 * by, 1)
        )

    def past(by):
        return place + by >= count

    by = 1
    while by < max(nx, ny):
        prod = prod * jnp.where(past(by), 1.0, against(prod, by))
        by *= 2
    weight = jnp.where(between, jnp.where(past(1), 1.0, against(prod, 1)), 0.0)

    def expand(width, per_block, species_of):
        src = iota((N, width), 0)
        col = iota((N, width), 1)
        hit = (src // 4 == col // per_block) & (src % 4 == species_of(col % per_block))
        return lax.dot_general(
            weight,
            jnp.where(hit, 1.0, 0.0),
            (((1,), (0,)), ((), ())),
            precision=lax.Precision.HIGHEST,
            preferred_element_type=f32,
        )

    width = nx * 16
    spread = expand(width, 16, lambda r: r // 4)
    rr, cc = iota((32, width), 0), iota((32, width), 1)
    wx[...] = jnp.where(
        rr % 16 == cc % 16, jnp.where(rr < 16, spread[0:1], spread[2:3]), 0.0
    )
    width = ny * 24
    spread = expand(width, 24, lambda r: jnp.where(r < 16, r // 4, r - 16))
    rr, cc = iota((40, width), 0), iota((40, width), 1)
    hit = jnp.where(rr < 32, rr % 16, 16 + rr % 4) == cc % 24
    left = (rr < 16) | ((rr >= 32) & (rr < 36))
    wy[...] = jnp.where(hit, jnp.where(left, spread[1:2], spread[3:4]), 0.0)

    lane1 = iota((1, N), 1)
    to_x = lax.rem(32 - 4 * k + N, N)
    to_y = lax.rem(36 - 4 * l + N, N)
    sx = pltpu.roll(slope, to_x, 1)
    sy = pltpu.roll(slope, to_y, 1)
    valid = (lane1 >= 32) & (lane1 < 40)
    sf = jnp.where(valid, jnp.where(lane1 < 36, sx[0:1], sy[1:2]), 1.0)
    sb = jnp.where(valid, jnp.where(lane1 < 36, sx[2:3], sy[3:4]), 1.0)
    phi = p0[...] + p1[...] * sf
    psi = q0[...] + q1[...] * sb
    phi_before, phi_after = 1.0 - sf, va + vb * sf
    psi_after, psi_before = 1.0 - sb, ua + ub * sb
    wron = sf * psi_before + (ca + cb * sb) * phi_before
    inv_w = 1.0 / wron
    psi = psi * inv_w
    psi_after, psi_before = psi_after * inv_w, psi_before * inv_w
    phi_t, psi_t = phi.T, psi.T
    eps = ey[...]
    eps_t = rows_y[...]
    i0, j0 = iota((N, N), 0), iota((N, N), 1)
    low = i0 >= j0
    r8 = iota((8, N), 0)
    c8 = iota((8, N), 1)
    for s in range(4):
        n = 32 + s
        e_b, e_a = eps_t[40 + s : 41 + s, N - 1 : N], eps_t[48 + s : 49 + s, 0:1]
        at = slice(n, n + 1)
        pr, qr = phi_t[at], psi_t[at]
        pc, qc, ec = phi[:, at], psi[:, at], eps[:, at]
        pb, pa, qb, qa = phi_before[:, at], phi_after[:, at], psi_before[:, at], psi_after[:, at]
        gx[s, 0:N, :] = jnp.where(low, (ec * qc) * pr, (ec * pc) * qr)
        gx[s, N:EXT, :] = jnp.where(
            r8 == 0, (e_b * pb) * qr, jnp.where(r8 == 1, (e_a * qa) * pr, 0.0)
        )
        lx[s, 0:N, :] = jnp.where(
            j0 == 0, ec * qc * pb, jnp.where(j0 == 1, ec * pc * qa, 0.0)
        )
        before = jnp.where(c8 == 0, e_b * pb * qb, e_b * pb * qa)
        after = jnp.where(c8 == 0, e_a * pb * qa, e_a * pa * qa)
        lx[s, N:EXT, :] = jnp.where(
            (r8 < 2) & (c8 < 2), jnp.where(r8 == 0, before, after), 0.0
        )
        hx[s] = jnp.where(
            r8 == 0, pr / pr[:, N - 1 : N], jnp.where(r8 == 1, qr / qr[:, 0:1], 0.0)
        )

        n = 36 + s
        e_b, e_a = eps_t[44 + s : 45 + s, N - 1 : N], eps_t[52 + s : 53 + s, 0:1]
        at = slice(n, n + 1)
        pr, qr, er = phi_t[at], psi_t[at], eps_t[at]
        pc, qc = phi[:, at], psi[:, at]
        pb, pa, qb, qa = phi_before[:, at], phi_after[:, at], psi_before[:, at], psi_after[:, at]
        gy[s, :, 0:N] = jnp.where(low, qc * (pr * er), pc * (qr * er))
        gy[s, :, N:] = jnp.where(
            j0 == 0, qc * (pb * e_b), jnp.where(j0 == 1, pc * (qa * e_a), 0.0)
        )
        ry[s, :, 0:N] = jnp.where(
            r8 == 0, pb * qr * er, jnp.where(r8 == 1, qa * pr * er, 0.0)
        )
        before = jnp.where(r8 == 0, e_b * pb * qb, e_b * pb * qa)
        after = jnp.where(r8 == 0, e_a * pb * qa, e_a * pa * qa)
        ry[s, :, N:] = jnp.where(
            (r8 < 2) & (c8 < 2), jnp.where(c8 == 0, before, after), 0.0
        )
        hy[s] = jnp.where(
            r8 == 0, pr / pr[:, N - 1 : N], jnp.where(r8 == 1, qr / qr[:, 0:1], 0.0)
        )


def edges_kernel(state, row_edges, col_edges):
    lane = iota((N, N), 1)
    cols = jnp.zeros((N, N), f32)
    for q in range(16):
        tile = state[q // 4, q % 4]
        row_edges[0, q : q + 1, :] = tile[0:1]
        row_edges[1, q : q + 1, :] = tile[N - 1 : N]
        cols = jnp.where(lane == q, tile[:, 0:1], cols)
        cols = jnp.where(lane == 16 + q, tile[:, N - 1 : N], cols)
    cols = cols.T
    col_edges[0] = cols[0:16]
    col_edges[1] = cols[16:32]


def explicit(tile_of, halo_of, rate, kin, cross, z, f_out):
    i0, j0 = iota((N, N), 0), iota((N, N), 1)
    tiles, laps = [], []
    for s in range(4):
        t = tile_of(s, z)
        up, down, left, right = halo_of(s, z)
        xm = jnp.where(i0 == 0, up, pltpu.roll(t, 1, 0))
        xp = jnp.where(i0 == N - 1, down, pltpu.roll(t, N - 1, 0))
        ym = jnp.where(j0 == 0, left, pltpu.roll(t, 1, 1))
        yp = jnp.where(j0 == N - 1, right, pltpu.roll(t, N - 1, 1))
        tiles.append(t)
        laps.append(xm + xp + ym + yp - 4.0 * t)
    for j in range(4):
        react = kin[0, j] * tiles[0]
        mix = cross[0, j] * laps[0]
        for i in range(1, 4):
            react = react + kin[i, j] * tiles[i]
            mix = mix + cross[i, j] * laps[i]
        f_out[j, :, z * N : (z + 1) * N] = (
            tiles[j] + 0.5 * rate[j, z] * react + 0.25 * mix
        )


def send_rows(f_out, hx, send, pay, nx):
    k = lax.axis_index("row")
    for s in range(4):
        ends = dot3(hx[s], f_out[s])
        for z in range(4):
            q = 4 * s + z
            pay[0, q : q + 1, :] = ends[0:1, z * N : (z + 1) * N]
            pay[1, q : q + 1, :] = ends[1:2, z * N : (z + 1) * N]
    a, b = pay[0], pay[1]
    for j in range(nx):
        send[j] = jnp.where(j > k, a, b)


def first_kernel(nx, state, rate, up, down, left, right, hx, kin, cross, f_out, send, cols, pay):
    zero = jnp.zeros((N - 32, N), f32)
    cols[...] = jnp.concatenate([left[...], right[...], zero], axis=0).T

    def halo_of(s, z):
        q = 4 * s + z
        return (
            up[q : q + 1, :],
            down[q : q + 1, :],
            cols[:, q : q + 1],
            cols[:, 16 + q : 17 + q],
        )

    for z in range(4):
        explicit(lambda s, z: state[s, z], halo_of, rate, kin, cross, z, f_out)
    send_rows(f_out, hx, send, pay, nx)


def rows_kernel(nx, ny, f_in, recv, wx, gx, lx, hy, g_out, send, pay):
    l = lax.axis_index("col")
    incoming = dot3(wx[...], recv[...].reshape(nx * 16, N))
    pay[...] = jnp.zeros_like(pay)
    for s in range(4):
        g = dot3(gx[s], f_in[s])
        lam, mu = lx[s, :, 0:1], lx[s, :, 1:2]
        parts, tails = [], []
        for z in range(4):
            q = 4 * s + z
            part = (
                g[:, z * N : (z + 1) * N]
                + lam * incoming[q : q + 1]
                + mu * incoming[16 + q : 17 + q]
            )
            g_out[s, z] = part
            parts.append(part[0:N])
            tails.append(part[N:EXT])
        ends = dot3(hy[s], jnp.concatenate(parts + tails, axis=0), nt=True)
        for p in range(2):
            for z in range(4):
                q = 4 * s + z
                pay[p, q : q + 1, :] = ends[p : p + 1, z * N : (z + 1) * N]
            pay[p, 16 + s : 17 + s, 0:32] = ends[p : p + 1, 4 * N : 4 * N + 32]
    a, b = pay[0], pay[1]
    for m in range(ny):
        send[m] = jnp.where(m > l, a, b)


def cols_part(ny, g_in, recv, wy, gy, ry, s, turned, wide):
    width = 2 * N if wide else N
    g = g_in[s].reshape(4 * EXT, N)
    out = dot3(g, gy[s, :, 0:width])
    lam, mu = ry[s, 0:1, 0:width], ry[s, 1:2, 0:width]
    result = []
    for z in range(4):
        q = 4 * s + z

        def column(p):
            main = turned[:, 16 * p + q : 16 * p + q + 1]
            tail = turned[8 * z : 8 * z + 8, 32 + 4 * p + s : 33 + 4 * p + s]
            return jnp.concatenate([main, tail], axis=0)

        result.append(
            out[z * EXT : (z + 1) * EXT] + column(0) * lam + column(1) * mu
        )
    return result


def turned_of(ny, recv, wy, turned):
    incoming = dot3(wy[...], recv[...].reshape(ny * 24, N))
    turned[...] = jnp.concatenate([incoming, jnp.zeros((N - 40, N), f32)], axis=0).T


def next_kernel(nx, ny, g_in, recv, wy, gy, ry, rate, hx, kin, cross, f_out, send, st, turned, pay):
    turned_of(ny, recv, wy, turned)
    for s in range(4):
        parts = cols_part(ny, g_in, recv, wy, gy, ry, s, turned, True)
        for z in range(4):
            st[s, z] = parts[z]

    def halo_of(s, z):
        return (
            st[s, z, N : N + 1, 0:N],
            st[s, z, N + 1 : N + 2, 0:N],
            st[s, z, 0:N, N : N + 1],
            st[s, z, 0:N, N + 1 : N + 2],
        )

    for z in range(4):
        explicit(lambda s, z: st[s, z, 0:N, 0:N], halo_of, rate, kin, cross, z, f_out)
    send_rows(f_out, hx, send, pay, nx)


def last_kernel(ny, g_in, recv, wy, gy, ry, out, turned):
    turned_of(ny, recv, wy, turned)
    for s in range(4):
        parts = cols_part(ny, g_in, recv, wy, gy, ry, s, turned, False)
        for z in range(4):
            out[s, z] = parts[z][0:N]


def call(body, outs, scratch, smem=0, cost=3_000_000):
    shapes = [jax.ShapeDtypeStruct(shape, f32) for shape in outs]

    def run(*args):
        count = len(args) - smem
        return pl.pallas_call(
            body,
            out_shape=shapes,
            in_specs=[pl.BlockSpec(memory_space=pltpu.VMEM)] * count
            + [pl.BlockSpec(memory_space=pltpu.SMEM)] * smem,
            out_specs=[pl.BlockSpec(memory_space=pltpu.VMEM)] * len(shapes),
            scratch_shapes=[pltpu.VMEM(shape, f32) for shape in scratch],
            compiler_params=pltpu.CompilerParams(vmem_limit_bytes=VMEM),
            cost_estimate=pl.CostEstimate(
                flops=cost * 1000, bytes_accessed=cost, transcendentals=0
            ),
        )(*args)

    return run


def on_device(adjoint, rate_scale, kinetics, cross_matrix, x_diffusion, y_diffusion):
    nx, ny = lax.axis_size("row"), lax.axis_size("col")
    row_edges, col_edges = call(edges_kernel, [(2, 16, N), (2, 16, N)], [])(adjoint)
    up = lax.ppermute(row_edges[1], "row", [(i, i + 1) for i in range(nx - 1)])
    down = lax.ppermute(row_edges[0], "row", [(i + 1, i) for i in range(nx - 1)])
    left = lax.ppermute(col_edges[1], "col", [(i, i + 1) for i in range(ny - 1)])
    right = lax.ppermute(col_edges[0], "col", [(i + 1, i) for i in range(ny - 1)])
    gx, lx, hx, gy, ry, hy, wx, wy = call(
        functools.partial(tables_kernel, nx, ny),
        [
            (4, EXT, N), (4, EXT, N), (4, 8, N), (4, N, 2 * N), (4, 8, 2 * N), (4, 8, N),
            (32, nx * 16), (40, ny * 24),
        ],
        [(N, N)] * 8,
    )(x_diffusion, y_diffusion)
    f_shape, g_shape = (4, N, 4 * N), (4, 4, EXT, N)
    send_x, send_y = (nx, 16, N), (ny, 24, N)
    f, send = call(
        functools.partial(first_kernel, nx), [f_shape, send_x], [(N, N), (2, 16, N)], 2
    )(adjoint, rate_scale, up, down, left, right, hx, kinetics, cross_matrix)
    for step in range(STEPS):
        recv = lax.all_to_all(send, "row", 0, 0, tiled=True)
        g, send = call(
            functools.partial(rows_kernel, nx, ny), [g_shape, send_y], [(2, 24, N)]
        )(f, recv, wx, gx, lx, hy)
        recv = lax.all_to_all(send, "col", 0, 0, tiled=True)
        if step + 1 < STEPS:
            f, send = call(
                functools.partial(next_kernel, nx, ny),
                [f_shape, send_x],
                [(4, 4, EXT, 2 * N), (N, N), (2, 16, N)],
                2,
            )(g, recv, wy, gy, ry, rate_scale, hx, kinetics, cross_matrix)
        else:
            (out,) = call(functools.partial(last_kernel, ny), [(4, 4, N, N)], [(N, N)])(
                g, recv, wy, gy, ry
            )
    return out


def solution(mesh):
    return jax.shard_map(
        on_device,
        mesh=mesh,
        in_specs=(P(None, None, "row", "col"), P(None, None, "row", "col"), P(), P(), P(), P()),
        out_specs=P(None, None, "row", "col"),
        check_vma=False,
    )
```

profile of v0, /device:TPU:1, one launch (start us, length us, event | category | flops | bytes accessed | tf_op | source)
XLA Modules:
  0.0 103.1 jit_solution(10419590182987917722)
XLA Ops:
  0.0 2.5 %shard_map.64 = (f32[2,16,128]{2,1,0:T(8,128)}, f32[2,16,128]{2,1,0:T(8,128)}) custom-call(f32[4,4,128,128]{3,2,1,0:T(8,128)} %state.3), custom_call_target="tpu_custom_call" | custom-call | flops 3000000000 | bytes 3000000 | tf_op jit(solution)/shard_map/pallas_call | solution.py:412
  2.5 0.7 slice_bitcast_fusion
  3.2 1.3 %collective-permute-start.3 = (f32[16,128]{1,0:T(8,128)S(1)}, f32[16,128]{1,0:T(8,128)S(1)}, u32[]{:S(2)}, u32[]{:S(2)}) collective-permute-start(f32[16,128]{1,0:T(8,128)S(1)} %get-tuple-element.41), channel_id=1, source_target_pairs={{1,0},{2,1},{3,2},{4,3},{5,4},{6,5},{7,6},{9,8},{10,9},{11,10},{12... | collective-permute-start | bytes 24584 | tf_op jit(solution)/shard_map/ppermute | solution.py:434
  4.5 5.0 %collective-permute-start.2 = (f32[16,128]{1,0:T(8,128)S(1)}, f32[16,128]{1,0:T(8,128)S(1)}, u32[]{:S(2)}, u32[]{:S(2)}) collective-permute-start(f32[16,128]{1,0:T(8,128)S(1)} %get-tuple-element.42), channel_id=1, source_target_pairs={{0,1},{1,2},{2,3},{3,4},{4,5},{5,6},{6,7},{8,9},{9,10},{10,11},{11... | collective-permute-start | bytes 24584 | tf_op jit(solution)/shard_map/ppermute | solution.py:433
  9.5 0.7 slice_bitcast_fusion.2
  10.3 4.7 %collective-permute-start.1 = (f32[16,128]{1,0:T(8,128)S(1)}, f32[16,128]{1,0:T(8,128)S(1)}, u32[]{:S(2)}, u32[]{:S(2)}) collective-permute-start(f32[16,128]{1,0:T(8,128)S(1)} %get-tuple-element.43), channel_id=1, source_target_pairs={{8,0},{16,8},{24,16},{32,24},{40,32},{48,40},{56,48},{64,56},{72,6... | collective-permute-start | bytes 24584 | tf_op jit(solution)/shard_map/ppermute | solution.py:432
  14.9 1.9 %collective-permute-start = (f32[16,128]{1,0:T(8,128)S(1)}, f32[16,128]{1,0:T(8,128)S(1)}, u32[]{:S(2)}, u32[]{:S(2)}) collective-permute-start(f32[16,128]{1,0:T(8,128)S(1)} %get-tuple-element.44), channel_id=1, source_target_pairs={{0,8},{8,16},{16,24},{24,32},{32,40},{40,48},{48,56},{56,64},{64,7... | collective-permute-start | bytes 24584 | tf_op jit(solution)/shard_map/ppermute | solution.py:431
  16.9 4.5 %shard_map.65 = (f32[4,136,128]{2,1,0:T(8,128)}, f32[4,136,128]{2,1,0:T(8,128)}, f32[4,8,128]{2,1,0:T(8,128)}, f32[4,128,256]{2,1,0:T(8,128)}, f32[4,8,256]{2,1,...) custom-call(f32[4,4096]{1,0:T(4,128)} %xd.1, f32[4,1024]{1,0:T(4,128)} %yd.1), custom_call_target="tpu_custom_call" | custom-call | flops 3000000000 | bytes 3000000 | tf_op jit(solution)/shard_map/pallas_call | solution.py:412
  21.4 0.0 collective-permute-done.3.right
  21.4 0.0 collective-permute-done.1.down
  21.4 0.0 collective-permute-done.up
  21.4 0.5 copy-done
  22.0 0.0 copy-done.1
  22.0 0.0 copy-done.2
  22.0 0.0 copy-done.3
  22.0 4.3 %shard_map.66 = (f32[4,128,512]{2,1,0:T(8,128)}, f32[32,16,128]{2,1,0:T(8,128)}) custom-call(f32[4,4,128,128]{3,2,1,0:T(8,128)} %state.3, f32[4,4,128,128]{3,2,1,0:T(8,128)} %rate.3, f32[16,128]{1,0:T(8,128)} %copy-done.3, f32[16,128]{1,0:T(8,128)} %copy-done.2, f32[16,128]{1,0:T(8,128)} %copy-done.1, f32[16,128]{1,0:T(8,128)} %copy-done, ...), custom_call_target="tpu_custom_call" | custom-call | flops 3000000000 | bytes 3000000 | tf_op jit(solution)/shard_map/pallas_call | solution.py:412
  26.4 17.0 %all_to_all.20.recv = f32[32,16,128]{2,1,0:T(8,128)} all-to-all(f32[32,16,128]{2,1,0:T(8,128)} %get-tuple-element.27), channel_id=1, replica_groups=mesh['row'=32,'col'=8] {'row'}, dimensions={0} | all-to-all | bytes 524288 | tf_op jit(solution)/shard_map/all_to_all | solution.py:449
  43.4 3.9 %shard_map.67 = (f32[4,4,136,128]{3,2,1,0:T(8,128)}, f32[8,24,128]{2,1,0:T(8,128)}) custom-call(f32[4,128,512]{2,1,0:T(8,128)} %get-tuple-element.26.f_in, f32[32,16,128]{2,1,0:T(8,128)} %all_to_all.20.recv, f32[32,512]{1,0:T(8,128)} %get-tuple-element.28.wx, f32[4,136,128]{2,1,0:T(8,128)} %get-tuple-element.29.gx, f32[4,136,128]{2,1,0:T(8,128)} %get-tuple-element.30.lx, ...), custom_call_target="tpu_custom_call" | custom-call | flops 3000000000 | bytes 3000000 | tf_op jit(solution)/shard_map/pallas_call | solution.py:412
  47.2 15.6 %all_to_all.21.recv = f32[8,24,128]{2,1,0:T(8,128)} all-to-all(f32[8,24,128]{2,1,0:T(8,128)} %get-tuple-element.33), channel_id=1, replica_groups=mesh['row'=32,'col'=8] {'col'}, dimensions={0} | all-to-all | bytes 196608 | tf_op jit(solution)/shard_map/all_to_all | solution.py:453
  62.8 6.0 %shard_map.68 = (f32[4,128,512]{2,1,0:T(8,128)}, f32[32,16,128]{2,1,0:T(8,128)}) custom-call(f32[4,4,136,128]{3,2,1,0:T(8,128)} %get-tuple-element.32.g_in, f32[8,24,128]{2,1,0:T(8,128)} %all_to_all.21.recv, f32[40,192]{1,0:T(8,128)} %get-tuple-element.34.wy, f32[4,128,256]{2,1,0:T(8,128)} %get-tuple-element.35.gy, f32[4,8,256]{2,1,0:T(8,128)} %get-tuple-element.36.ry, ...), custom_call_target="tpu_custom_call" | custom-call | flops 3000000000 | bytes 3000000 | tf_op jit(solution)/shard_map/pallas_call | solution.py:412
  68.8 15.1 %all_to_all.22.recv = f32[32,16,128]{2,1,0:T(8,128)} all-to-all(f32[32,16,128]{2,1,0:T(8,128)} %get-tuple-element.38), channel_id=1, replica_groups=mesh['row'=32,'col'=8] {'row'}, dimensions={0} | all-to-all | bytes 524288 | tf_op jit(solution)/shard_map/all_to_all | solution.py:449
  84.0 3.8 %shard_map.69 = (f32[4,4,136,128]{3,2,1,0:T(8,128)}, f32[8,24,128]{2,1,0:T(8,128)}) custom-call(f32[4,128,512]{2,1,0:T(8,128)} %get-tuple-element.37.f_in, f32[32,16,128]{2,1,0:T(8,128)} %all_to_all.22.recv, f32[32,512]{1,0:T(8,128)} %get-tuple-element.28.wx, f32[4,136,128]{2,1,0:T(8,128)} %get-tuple-element.29.gx, f32[4,136,128]{2,1,0:T(8,128)} %get-tuple-element.30.lx, ...), custom_call_target="tpu_custom_call" | custom-call | flops 3000000000 | bytes 3000000 | tf_op jit(solution)/shard_map/pallas_call | solution.py:412
  87.8 11.8 %all_to_all.23.recv = f32[8,24,128]{2,1,0:T(8,128)} all-to-all(f32[8,24,128]{2,1,0:T(8,128)} %get-tuple-element.40), channel_id=1, replica_groups=mesh['row'=32,'col'=8] {'col'}, dimensions={0} | all-to-all | bytes 196608 | tf_op jit(solution)/shard_map/all_to_all | solution.py:453
  99.6 3.5 %shard_map.70 = f32[4,4,128,128]{3,2,1,0:T(8,128)} custom-call(f32[4,4,136,128]{3,2,1,0:T(8,128)} %get-tuple-element.39.g_in, f32[8,24,128]{2,1,0:T(8,128)} %all_to_all.23.recv, f32[40,192]{1,0:T(8,128)} %get-tuple-element.34.wy, f32[4,128,256]{2,1,0:T(8,128)} %get-tuple-element.35.gy, f32[4,8,256]{2,1,0:T(8,128)} %get-tuple-element.36.ry), custom_call_target="tpu_custom_call" | custom-call | flops 3000000000 | bytes 3000000 | tf_op jit(solution)/shard_map/pallas_call | solution.py:412
  (5 shorter events, 0.0 us)
Async XLA Ops:
  3.2 18.1 %collective-permute-start.3 = (f32[16,128]{1,0:T(8,128)S(1)}, f32[16,128]{1,0:T(8,128)S(1)}, u32[]{:S(2)}, u32[]{:S(2)}) collective-permute-start(f32[16,128]{1,0:T(8,128)S(1)} %get-tuple-element.41), channel_id=1, source_target_pairs={{1,0},{2,1},{3,2},{4,3},{5,4},{6,5},{7,6},{9,8},{10,9},{11,10},{12... | collective-permute-start | bytes 24584 | tf_op jit(solution)/shard_map/ppermute | solution.py:434
  4.5 16.9 %collective-permute-start.2 = (f32[16,128]{1,0:T(8,128)S(1)}, f32[16,128]{1,0:T(8,128)S(1)}, u32[]{:S(2)}, u32[]{:S(2)}) collective-permute-start(f32[16,128]{1,0:T(8,128)S(1)} %get-tuple-element.42), channel_id=1, source_target_pairs={{0,1},{1,2},{2,3},{3,4},{4,5},{5,6},{6,7},{8,9},{9,10},{10,11},{11... | collective-permute-start | bytes 24584 | tf_op jit(solution)/shard_map/ppermute | solution.py:433
  10.3 11.2 %collective-permute-start.1 = (f32[16,128]{1,0:T(8,128)S(1)}, f32[16,128]{1,0:T(8,128)S(1)}, u32[]{:S(2)}, u32[]{:S(2)}) collective-permute-start(f32[16,128]{1,0:T(8,128)S(1)} %get-tuple-element.43), channel_id=1, source_target_pairs={{8,0},{16,8},{24,16},{32,24},{40,32},{48,40},{56,48},{64,56},{72,6... | collective-permute-start | bytes 24584 | tf_op jit(solution)/shard_map/ppermute | solution.py:432
  14.9 6.5 %collective-permute-start = (f32[16,128]{1,0:T(8,128)S(1)}, f32[16,128]{1,0:T(8,128)S(1)}, u32[]{:S(2)}, u32[]{:S(2)}) collective-permute-start(f32[16,128]{1,0:T(8,128)S(1)} %get-tuple-element.44), channel_id=1, source_target_pairs={{0,8},{8,16},{16,24},{24,32},{32,40},{40,48},{48,56},{56,64},{64,7... | collective-permute-start | bytes 24584 | tf_op jit(solution)/shard_map/ppermute | solution.py:431
  21.4 0.6 copy-start
  21.4 0.6 copy-start.1
  21.4 0.6 copy-start.2
  21.4 0.6 copy-start.3
where the time goes:
time: 104 us; the launch traced here: 103 us
  blocking collectives  59.5 us (57%)
  Pallas kernels  28.6 us (28%)
  starting transfers between devices  12.9 us (12%)
  local copies, waits for them, and re-layouts  2.03 us (2%)
    all_to_all x2, blocking collectives, on_device(): recv = lax.all_to_all(send, 'row', 0, 0, tiled=True)  32.1 us
    pallas_call x7, Pallas kernels, run(): pl.pallas_call(body, out_shape=shapes, in_specs=[pl.BlockSpec(memory_spac...  28.6 us
    all_to_all x2, blocking collectives, on_device(): recv = lax.all_to_all(send, 'col', 0, 0, tiled=True)  27.4 us
    ppermute x1, starting transfers between devices, on_device(): lax.ppermute(col_edges[1], 'col', [(i, i + 1) for i in range(ny - 1)])  5 us
    ppermute x1, starting transfers between devices, on_device(): lax.ppermute(row_edges[0], 'row', [(i + 1, i) for i in range(nx - 1)])  4.68 us
  transfers between devices with their start and end apart: 4, of which 0 were waited for; matrix products, arithmetic and copies ran while one was open for 1% of the time, Pallas kernels for 4%

commit v1 on v0

--- a/solution.py
+++ b/solution.py
@@ -13,7 +13,7 @@
 EXT = N + 8
 f32 = jnp.float32
 bf16 = jnp.bfloat16
-VMEM = 56 * 1024 * 1024
+VMEM = 20 * 1024 * 1024
 
 
 def iota(shape, dim):

time: 104 us -> 86.6 us (0.83)
  Pallas kernels: 28.6 us -> 15.5 us
  blocking collectives: 59.5 us -> 56.2 us
    pallas_call x7, Pallas kernels: 28.6 us -> 15.5 us  [run(): pl.pallas_call(body, out_shape=shapes, in_specs=[pl.BlockSpec(memory_spac...]
    all_to_all x2, blocking collectives: 27.4 us -> 25.5 us  [on_device(): recv = lax.all_to_all(send, 'col', 0, 0, tiled=True)]
    all_to_all x2, blocking collectives: 32.1 us -> 30.7 us  [on_device(): recv = lax.all_to_all(send, 'row', 0, 0, tiled=True)]
  transfers between devices with their start and end apart: 4 -> 4, of which waited for: 0 -> 0; matrix products, arithmetic and copies ran while one was open for 1% -> 0% of each run, Pallas kernels for 4% -> 3%
where the time goes in v1:
time: 86.6 us; the launch traced here: 86.2 us
  blocking collectives  56.2 us (65%)
  Pallas kernels  15.5 us (18%)
  starting transfers between devices  13 us (15%)
  local copies, waits for them, and re-layouts  1.27 us (1%)
    all_to_all x2, blocking collectives, on_device(): recv = lax.all_to_all(send, 'row', 0, 0, tiled=True)  30.7 us
    all_to_all x2, blocking collectives, on_device(): recv = lax.all_to_all(send, 'col', 0, 0, tiled=True)  25.5 us
    pallas_call x7, Pallas kernels, run(): pl.pallas_call(body, out_shape=shapes, in_specs=[pl.BlockSpec(memory_spac...  15.5 us
    ppermute x1, starting transfers between devices, on_device(): lax.ppermute(col_edges[1], 'col', [(i, i + 1) for i in range(ny - 1)])  5 us
    ppermute x1, starting transfers between devices, on_device(): lax.ppermute(row_edges[0], 'row', [(i + 1, i) for i in range(nx - 1)])  4.7 us
    ppermute x1, starting transfers between devices, on_device(): up = lax.ppermute(row_edges[1], 'row', [(i, i + 1) for i in range(nx - 1)])  2.05 us
  transfers between devices with their start and end apart: 4, of which 0 were waited for; matrix products, arithmetic and copies ran while one was open for 0% of the time, Pallas kernels for 3%

profile of v1, /device:TPU:1, one launch (start us, length us, event | category | flops | bytes accessed | tf_op | source)
XLA Modules:
  0.0 86.2 jit_solution(1379758765849483107)
XLA Ops:
  0.0 1.2 %copy-done = f32[4,4,128,128]{3,2,1,0:T(8,128)S(1)} copy-done((f32[4,4,128,128]{3,2,1,0:T(8,128)S(1)}, f32[4,4,128,128]{3,2,1,0:T(8,128)}, u32[]{:S(2)}) %copy-start) | copy-done | bytes 1048600
  1.2 0.7 shard_map.64
  1.9 1.3 %collective-permute-start.3 = (f32[16,128]{1,0:T(8,128)S(1)}, f32[16,128]{1,0:T(8,128)S(1)}, u32[]{:S(2)}, u32[]{:S(2)}) collective-permute-start(f32[16,128]{1,0:T(8,128)S(1)} %get-tuple-element.41), channel_id=1, source_target_pairs={{1,0},{2,1},{3,2},{4,3},{5,4},{6,5},{7,6},{9,8},{10,9},{11,10},{12... | collective-permute-start | bytes 24584 | tf_op jit(solution)/shard_map/ppermute | solution.py:434
  3.2 5.0 %collective-permute-start.2 = (f32[16,128]{1,0:T(8,128)S(1)}, f32[16,128]{1,0:T(8,128)S(1)}, u32[]{:S(2)}, u32[]{:S(2)}) collective-permute-start(f32[16,128]{1,0:T(8,128)S(1)} %get-tuple-element.42), channel_id=1, source_target_pairs={{0,1},{1,2},{2,3},{3,4},{4,5},{5,6},{6,7},{8,9},{9,10},{10,11},{11... | collective-permute-start | bytes 24584 | tf_op jit(solution)/shard_map/ppermute | solution.py:433
  8.2 4.7 %collective-permute-start.1 = (f32[16,128]{1,0:T(8,128)S(1)}, f32[16,128]{1,0:T(8,128)S(1)}, u32[]{:S(2)}, u32[]{:S(2)}) collective-permute-start(f32[16,128]{1,0:T(8,128)S(1)} %get-tuple-element.43), channel_id=1, source_target_pairs={{8,0},{16,8},{24,16},{32,24},{40,32},{48,40},{56,48},{64,56},{72,6... | collective-permute-start | bytes 24584 | tf_op jit(solution)/shard_map/ppermute | solution.py:432
  13.0 0.0 copy-start.1
  13.0 0.0 copy-start.2
  13.0 0.0 copy-start.5
  13.0 0.0 copy-start.6
  13.0 2.1 %collective-permute-start = (f32[16,128]{1,0:T(8,128)S(1)}, f32[16,128]{1,0:T(8,128)S(1)}, u32[]{:S(2)}, u32[]{:S(2)}) collective-permute-start(f32[16,128]{1,0:T(8,128)S(1)} %get-tuple-element.44), channel_id=1, source_target_pairs={{0,8},{8,16},{16,24},{24,32},{32,40},{40,48},{48,56},{56,64},{64,7... | collective-permute-start | bytes 24584 | tf_op jit(solution)/shard_map/ppermute | solution.py:431
  15.1 2.8 %shard_map.65 = (f32[4,136,128]{2,1,0:T(8,128)S(1)}, f32[4,136,128]{2,1,0:T(8,128)S(1)}, f32[4,8,128]{2,1,0:T(8,128)S(1)}, f32[4,128,256]{2,1,0:T(8,128)S(1)}, f...) custom-call(f32[4,4096]{1,0:T(4,128)S(1)} %copy-done.3, ...), custom_call_target="tpu_custom_call" | custom-call | flops 3000000000 | bytes 3000000 | tf_op jit(solution)/shard_map/pallas_call | solution.py:412
  17.9 0.0 collective-permute-done.3.right
  17.9 0.0 collective-permute-done.2.left
  17.9 0.0 collective-permute-done.1.down
  17.9 0.0 collective-permute-done.up
  17.9 2.7 %shard_map.66 = (f32[4,128,512]{2,1,0:T(8,128)S(1)}, f32[32,16,128]{2,1,0:T(8,128)S(1)}) custom-call(f32[4,4,128,128]{3,2,1,0:T(8,128)S(1)} %copy-done.1, f32[4,4,128,128]{3,2,1,0:T(8,128)S(1)} %copy-done.2, f32[16,128]{1,0:T(8,128)S(1)} %collective-permute-done.up, f32[16,128]{1,0:T(8,128)S(1)} %collective-permute-done.1.down, ...), custom_call_target="tpu_custom_call" | custom-call | flops 3000000000 | bytes 3000000 | tf_op jit(solution)/shard_map/pallas_call | solution.py:412
  20.7 16.7 %all_to_all.20.recv = f32[32,16,128]{2,1,0:T(8,128)S(1)} all-to-all(f32[32,16,128]{2,1,0:T(8,128)S(1)} %get-tuple-element.27), channel_id=1, replica_groups=mesh['row'=32,'col'=8] {'row'}, dimensions={0} | all-to-all | bytes 524288 | tf_op jit(solution)/shard_map/all_to_all | solution.py:449
  37.4 1.6 %shard_map.67 = (f32[4,4,136,128]{3,2,1,0:T(8,128)S(1)}, f32[8,24,128]{2,1,0:T(8,128)S(1)}) custom-call(f32[4,128,512]{2,1,0:T(8,128)S(1)} %get-tuple-element.26.f_in, f32[32,16,128]{2,1,0:T(8,128)S(1)} %all_to_all.20.recv, f32[32,512]{1,0:T(8,128)S(1)} %get-tuple-element.28.wx, f32[4,136,128]{2,1,0:T(8,128)S(1)} %get-tuple-element.29.gx, ...), custom_call_target="tpu_custom_call" | custom-call | flops 3000000000 | bytes 3000000 | tf_op jit(solution)/shard_map/pallas_call | solution.py:412
  39.0 15.3 %all_to_all.21.recv = f32[8,24,128]{2,1,0:T(8,128)S(1)} all-to-all(f32[8,24,128]{2,1,0:T(8,128)S(1)} %get-tuple-element.33), channel_id=1, replica_groups=mesh['row'=32,'col'=8] {'col'}, dimensions={0} | all-to-all | bytes 196608 | tf_op jit(solution)/shard_map/all_to_all | solution.py:453
  54.2 4.1 %shard_map.68 = (f32[4,128,512]{2,1,0:T(8,128)S(1)}, f32[32,16,128]{2,1,0:T(8,128)S(1)}) custom-call(f32[4,4,136,128]{3,2,1,0:T(8,128)S(1)} %get-tuple-element.32.g_in, f32[8,24,128]{2,1,0:T(8,128)S(1)} %all_to_all.21.recv, f32[40,192]{1,0:T(8,128)S(1)} %get-tuple-element.34.wy, f32[4,128,256]{2,1,0:T(8,128)S(1)} %get-tuple-element.35.gy, ...), custom_call_target="tpu_custom_call" | custom-call | flops 3000000000 | bytes 3000000 | tf_op jit(solution)/shard_map/pallas_call | solution.py:412
  58.3 14.0 %all_to_all.22.recv = f32[32,16,128]{2,1,0:T(8,128)S(1)} all-to-all(f32[32,16,128]{2,1,0:T(8,128)S(1)} %get-tuple-element.38), channel_id=1, replica_groups=mesh['row'=32,'col'=8] {'row'}, dimensions={0} | all-to-all | bytes 524288 | tf_op jit(solution)/shard_map/all_to_all | solution.py:449
  72.4 1.6 %shard_map.69 = (f32[4,4,136,128]{3,2,1,0:T(8,128)S(1)}, f32[8,24,128]{2,1,0:T(8,128)S(1)}) custom-call(f32[4,128,512]{2,1,0:T(8,128)S(1)} %get-tuple-element.37.f_in, f32[32,16,128]{2,1,0:T(8,128)S(1)} %all_to_all.22.recv, f32[32,512]{1,0:T(8,128)S(1)} %get-tuple-element.28.wx, f32[4,136,128]{2,1,0:T(8,128)S(1)} %get-tuple-element.29.gx, ...), custom_call_target="tpu_custom_call" | custom-call | flops 3000000000 | bytes 3000000 | tf_op jit(solution)/shard_map/pallas_call | solution.py:412
  73.9 10.3 %all_to_all.23.recv = f32[8,24,128]{2,1,0:T(8,128)S(1)} all-to-all(f32[8,24,128]{2,1,0:T(8,128)S(1)} %get-tuple-element.40), channel_id=1, replica_groups=mesh['row'=32,'col'=8] {'col'}, dimensions={0} | all-to-all | bytes 196608 | tf_op jit(solution)/shard_map/all_to_all | solution.py:453
  84.2 2.0 %shard_map.70 = f32[4,4,128,128]{3,2,1,0:T(8,128)} custom-call(f32[4,4,136,128]{3,2,1,0:T(8,128)S(1)} %get-tuple-element.39.g_in, f32[8,24,128]{2,1,0:T(8,128)S(1)} %all_to_all.23.recv, f32[40,192]{1,0:T(8,128)S(1)} %get-tuple-element.34.wy, f32[4,128,256]{2,1,0:T(8,128)S(1)} %get-tuple-element.35.gy, f32[4,8,256]{2,1,0:T(8,128)S(1)} %get-tuple-element.36.ry), custom_call_target="tpu_custom_call" | custom-call | flops 3000000000 | bytes 3000000 | tf_op jit(solution)/shard_map/pallas_call | solution.py:412
  (11 shorter events, 0.0 us)
Async XLA Ops:
  0.0 1.2 %copy-start = (f32[4,4,128,128]{3,2,1,0:T(8,128)S(1)}, f32[4,4,128,128]{3,2,1,0:T(8,128)}, u32[]{:S(2)}) copy-start(f32[4,4,128,128]{3,2,1,0:T(8,128)} %state.3) | copy-start | bytes 3145732
  1.2 13.8 %copy-start.3 = (f32[4,4096]{1,0:T(4,128)S(1)}, f32[4,4096]{1,0:T(4,128)}, u32[]{:S(2)}) copy-start(f32[4,4096]{1,0:T(4,128)} %xd.1) | copy-start | bytes 196612
  1.2 13.8 %copy-start.4 = (f32[4,1024]{1,0:T(4,128)S(1)}, f32[4,1024]{1,0:T(4,128)}, u32[]{:S(2)}) copy-start(f32[4,1024]{1,0:T(4,128)} %yd.1) | copy-start | bytes 49156
  1.9 15.9 %collective-permute-start.3 = (f32[16,128]{1,0:T(8,128)S(1)}, f32[16,128]{1,0:T(8,128)S(1)}, u32[]{:S(2)}, u32[]{:S(2)}) collective-permute-start(f32[16,128]{1,0:T(8,128)S(1)} %get-tuple-element.41), channel_id=1, source_target_pairs={{1,0},{2,1},{3,2},{4,3},{5,4},{6,5},{7,6},{9,8},{10,9},{11,10},{12... | collective-permute-start | bytes 24584 | tf_op jit(solution)/shard_map/ppermute | solution.py:434
  3.2 14.7 %collective-permute-start.2 = (f32[16,128]{1,0:T(8,128)S(1)}, f32[16,128]{1,0:T(8,128)S(1)}, u32[]{:S(2)}, u32[]{:S(2)}) collective-permute-start(f32[16,128]{1,0:T(8,128)S(1)} %get-tuple-element.42), channel_id=1, source_target_pairs={{0,1},{1,2},{2,3},{3,4},{4,5},{5,6},{6,7},{8,9},{9,10},{10,11},{11... | collective-permute-start | bytes 24584 | tf_op jit(solution)/shard_map/ppermute | solution.py:433
  8.2 9.6 %collective-permute-start.1 = (f32[16,128]{1,0:T(8,128)S(1)}, f32[16,128]{1,0:T(8,128)S(1)}, u32[]{:S(2)}, u32[]{:S(2)}) collective-permute-start(f32[16,128]{1,0:T(8,128)S(1)} %get-tuple-element.43), channel_id=1, source_target_pairs={{8,0},{16,8},{24,16},{32,24},{40,32},{48,40},{56,48},{64,56},{72,6... | collective-permute-start | bytes 24584 | tf_op jit(solution)/shard_map/ppermute | solution.py:432
  13.0 5.0 %copy-start.1 = (f32[4,4,128,128]{3,2,1,0:T(8,128)S(1)}, f32[4,4,128,128]{3,2,1,0:T(8,128)}, u32[]{:S(2)}) copy-start(f32[4,4,128,128]{3,2,1,0:T(8,128)} %state.3) | copy-start | bytes 3145732
  13.0 5.0 %copy-start.2 = (f32[4,4,128,128]{3,2,1,0:T(8,128)S(1)}, f32[4,4,128,128]{3,2,1,0:T(8,128)}, u32[]{:S(2)}) copy-start(f32[4,4,128,128]{3,2,1,0:T(8,128)} %rate.3) | copy-start | bytes 3145732
  13.0 5.0 %copy-start.5 = (f32[4,4]{1,0:T(4,128)S(1)}, f32[4,4]{1,0:T(4,128)}, u32[]{:S(2)}) copy-start(f32[4,4]{1,0:T(4,128)} %kin.3) | copy-start | bytes 196
  13.0 5.0 %copy-start.6 = (f32[4,4]{1,0:T(4,128)S(1)}, f32[4,4]{1,0:T(4,128)}, u32[]{:S(2)}) copy-start(f32[4,4]{1,0:T(4,128)} %cross.3) | copy-start | bytes 196
  13.0 4.9 %collective-permute-start = (f32[16,128]{1,0:T(8,128)S(1)}, f32[16,128]{1,0:T(8,128)S(1)}, u32[]{:S(2)}, u32[]{:S(2)}) collective-permute-start(f32[16,128]{1,0:T(8,128)S(1)} %get-tuple-element.44), channel_id=1, source_target_pairs={{0,8},{8,16},{16,24},{24,32},{32,40},{40,48},{48,56},{56,64},{64,7... | collective-permute-start | bytes 24584 | tf_op jit(solution)/shard_map/ppermute | solution.py:431

commit v2 on v1

--- a/solution.py
+++ b/solution.py
@@ -7,7 +7,6 @@
 from jax.experimental.pallas import tpu as pltpu
 from jax.sharding import PartitionSpec as P
 
-STEPS = 2
 M = 1000.0
 N = 128
 EXT = N + 8
@@ -37,7 +36,7 @@
 
 
 def tables_kernel(
-    nx, ny, xd, yd, gx, lx, hx, gy, ry, hy, wx, wy,
+    nx, ny, xd, yd, gx, lx, hx, gy, ry, hy, wx, wx_cols, wy, wy_last,
     rows_x, rows_y, ex, ey, p0, p1, q0, q1,
 ):
     k = lax.axis_index("row")
@@ -178,12 +177,25 @@
     wx[...] = jnp.where(
         rr % 16 == cc % 16, jnp.where(rr < 16, spread[0:1], spread[2:3]), 0.0
     )
+    width = nx * 8
+    spread = expand(width, 8, lambda r: r)
+    rr, cc = iota((16, width), 0), iota((16, width), 1)
+    wx_cols[...] = jnp.where(
+        rr % 8 == cc % 8, jnp.where(rr < 8, spread[0:1], spread[2:3]), 0.0
+    )
     width = ny * 24
     spread = expand(width, 24, lambda r: jnp.where(r < 16, r // 4, r - 16))
-    rr, cc = iota((40, width), 0), iota((40, width), 1)
-    hit = jnp.where(rr < 32, rr % 16, 16 + rr % 4) == cc % 24
-    left = (rr < 16) | ((rr >= 32) & (rr < 36))
+    rr, cc = iota((48, width), 0), iota((48, width), 1)
+    hit = jnp.where(rr < 32, rr % 16, 16 + rr % 8) == cc % 24
+    left = (rr < 16) | ((rr >= 32) & (rr < 40))
     wy[...] = jnp.where(hit, jnp.where(left, spread[1:2], spread[3:4]), 0.0)
+
+    width = ny * 16
+    spread = expand(width, 16, lambda r: r // 4)
+    rr, cc = iota((32, width), 0), iota((32, width), 1)
+    wy_last[...] = jnp.where(
+        rr % 16 == cc % 16, jnp.where(rr < 16, spread[1:2], spread[3:4]), 0.0
+    )
 
     lane1 = iota((1, N), 1)
     to_x = lax.rem(32 - 4 * k + N, N)
@@ -227,8 +239,16 @@
         lx[s, N:EXT, :] = jnp.where(
             (r8 < 2) & (c8 < 2), jnp.where(r8 == 0, before, after), 0.0
         )
+        inv_p, inv_q = 1.0 / pr[:, N - 1 : N], 1.0 / qr[:, 0:1]
+        beside = jnp.where(
+            c8 == 0,
+            pb * inv_p,
+            jnp.where(c8 == 1, pa * inv_p, jnp.where(c8 == 2, qb * inv_q, qa * inv_q)),
+        )
         hx[s] = jnp.where(
-            r8 == 0, pr / pr[:, N - 1 : N], jnp.where(r8 == 1, qr / qr[:, 0:1], 0.0)
+            r8 == 0,
+            pr * inv_p,
+            jnp.where(r8 == 1, qr * inv_q, jnp.where(r8 == 2, beside, 0.0)),
         )
 
         n = 36 + s
@@ -249,23 +269,21 @@
         ry[s, :, N:] = jnp.where(
             (r8 < 2) & (c8 < 2), jnp.where(c8 == 0, before, after), 0.0
         )
-        hy[s] = jnp.where(
-            r8 == 0, pr / pr[:, N - 1 : N], jnp.where(r8 == 1, qr / qr[:, 0:1], 0.0)
-        )
-
-
-def edges_kernel(state, row_edges, col_edges):
-    lane = iota((N, N), 1)
-    cols = jnp.zeros((N, N), f32)
-    for q in range(16):
-        tile = state[q // 4, q % 4]
-        row_edges[0, q : q + 1, :] = tile[0:1]
-        row_edges[1, q : q + 1, :] = tile[N - 1 : N]
-        cols = jnp.where(lane == q, tile[:, 0:1], cols)
-        cols = jnp.where(lane == 16 + q, tile[:, N - 1 : N], cols)
-    cols = cols.T
-    col_edges[0] = cols[0:16]
-    col_edges[1] = cols[16:32]
+        inv_p, inv_q = 1.0 / pr[:, N - 1 : N], 1.0 / qr[:, 0:1]
+        hy[s, :, 0:N] = jnp.where(
+            r8 < 4, jnp.where(r8 % 2 == 0, pr * inv_p, qr * inv_q), 0.0
+        )
+        before = jnp.where(
+            (r8 == 0) | (r8 == 2),
+            pb * inv_p,
+            jnp.where(r8 == 3, qb * inv_q, jnp.where(r8 == 4, 1.0, 0.0)),
+        )
+        after = jnp.where(
+            (r8 == 1) | (r8 == 3),
+            qa * inv_q,
+            jnp.where(r8 == 2, pa * inv_p, jnp.where(r8 == 5, 1.0, 0.0)),
+        )
+        hy[s, :, N:] = jnp.where(c8 == 0, before, jnp.where(c8 == 1, after, 0.0))
 
 
 def explicit(tile_of, halo_of, rate, kin, cross, z, f_out):
@@ -291,35 +309,130 @@
         )
 
 
+def line_sums(f_out, hx, s):
+    ends = dot3(hx[s], f_out[s])
+    return ends[0:1], ends[1:2]
+
+
+def by_plane(ref, p, s, values):
+    for z in range(4):
+        q = 4 * s + z
+        ref[p, q : q + 1, :] = values[:, z * N : (z + 1) * N]
+
+
 def send_rows(f_out, hx, send, pay, nx):
     k = lax.axis_index("row")
     for s in range(4):
-        ends = dot3(hx[s], f_out[s])
+        a, b = line_sums(f_out, hx, s)
+        by_plane(pay, 0, s, a)
+        by_plane(pay, 1, s, b)
+    for j in range(nx):
+        send[j] = pay[(j < k).astype(jnp.int32)]
+
+
+def message(j, own):
+    return jnp.where(j > own, 0, 1) + jnp.where((j == own + 1) | (j == own - 1), 0, 2)
+
+
+def first_kernel(nx, ny, state, rate, hx, kin, cross, f_out, send, cells, cols, pay):
+    k, l = lax.axis_index("row"), lax.axis_index("col")
+    none = (0.0, 0.0, 0.0, 0.0)
+    for z in range(4):
+        explicit(lambda s, z: state[s, z], lambda s, z: none, rate, kin, cross, z, f_out)
+
+    lane = iota((N, N), 1)
+    side = []
+    for s in range(4):
+        acc = jnp.zeros((N, N), f32)
         for z in range(4):
-            q = 4 * s + z
-            pay[0, q : q + 1, :] = ends[0:1, z * N : (z + 1) * N]
-            pay[1, q : q + 1, :] = ends[1:2, z * N : (z + 1) * N]
-    a, b = pay[0], pay[1]
+            tile = state[s, z]
+            acc = jnp.where(lane == 8 * z, tile[:, 0:1], acc)
+            acc = jnp.where(lane == 8 * z + 1, tile[:, N - 1 : N], acc)
+        side.append(acc)
+    has = jnp.where(lane % 8 == 0, (l > 0).astype(f32), (l < ny - 1).astype(f32))
+    before_x = 0.25 * (k > 0).astype(f32)
+    after_x = 0.25 * (k < nx - 1).astype(f32)
+    pay[...] = jnp.zeros_like(pay)
+    for j in range(4):
+        mix = cross[0, j] * side[0]
+        for i in range(1, 4):
+            mix = mix + cross[i, j] * side[i]
+        mix = 0.25 * has * mix
+        cols[j] = mix
+        for z in range(4):
+            q = 4 * j + z
+            low = cross[0, j] * state[0, z, 0:1, :]
+            high = cross[0, j] * state[0, z, N - 1 : N, :]
+            for i in range(1, 4):
+                low = low + cross[i, j] * state[i, z, 0:1, :]
+                high = high + cross[i, j] * state[i, z, N - 1 : N, :]
+            cells[0, q : q + 1, :] = before_x * low
+            cells[1, q : q + 1, :] = after_x * high
+        a, b = line_sums(f_out, hx, j)
+        before = jnp.concatenate([cells[0, 4 * j + z : 4 * j + z + 1, :] for z in range(4)], axis=1)
+        after = jnp.concatenate([cells[1, 4 * j + z : 4 * j + z + 1, :] for z in range(4)], axis=1)
+        p_b, p_a = hx[j, 2:3, 0:1], hx[j, 2:3, 1:2]
+        q_b, q_a = hx[j, 2:3, 2:3], hx[j, 2:3, 3:4]
+        a = a + p_b * before
+        b = b + q_a * after
+        by_plane(pay, 0, j, a)
+        by_plane(pay, 1, j, b)
+        by_plane(pay, 2, j, a + p_a * after)
+        by_plane(pay, 3, j, b + q_b * before)
+        ends = dot3(hx[j], mix)
+        for p in range(4):
+            pay[p, 32 + j : 33 + j, :] = ends[p % 2 : p % 2 + 1]
+    for p in range(4):
+        pay[p, 16:32, :] = cells[1 - p % 2]
     for j in range(nx):
-        send[j] = jnp.where(j > k, a, b)
-
-
-def first_kernel(nx, state, rate, up, down, left, right, hx, kin, cross, f_out, send, cols, pay):
-    zero = jnp.zeros((N - 32, N), f32)
-    cols[...] = jnp.concatenate([left[...], right[...], zero], axis=0).T
-
-    def halo_of(s, z):
-        q = 4 * s + z
-        return (
-            up[q : q + 1, :],
-            down[q : q + 1, :],
-            cols[:, q : q + 1],
-            cols[:, 16 + q : 17 + q],
-        )
-
-    for z in range(4):
-        explicit(lambda s, z: state[s, z], halo_of, rate, kin, cross, z, f_out)
-    send_rows(f_out, hx, send, pay, nx)
+        send[j] = pay[message(j, k)]
+
+
+def first_rows_kernel(
+    nx, ny, f_in, cells, cols, recv, wx, wx_cols, gx, lx, hy, g_out, send, beside, pay
+):
+    k, l = lax.axis_index("row"), lax.axis_index("col")
+    incoming = dot3(wx[...], recv[:, 0:16, :].reshape(nx * 16, N))
+    in_cols = dot3(wx_cols[...], recv[:, 32:40, :].reshape(nx * 8, N))
+    from_before = incoming[0:16] + cells[0]
+    from_after = incoming[16:32] + cells[1]
+    at_first = recv[jnp.maximum(k - 1, 0), 16:32, :] * (k > 0).astype(f32)
+    at_last = recv[jnp.minimum(k + 1, nx - 1), 16:32, :] * (k < nx - 1).astype(f32)
+    pay[...] = jnp.zeros_like(pay)
+    for s in range(4):
+        g = dot3(gx[s], f_in[s])
+        lam, mu = lx[s, :, 0:1], lx[s, :, 1:2]
+        col = (
+            dot3(gx[s], cols[s])
+            + lam * in_cols[s : s + 1]
+            + mu * in_cols[8 + s : 9 + s]
+        )
+        first, last = gx[s, :, 0:1], gx[s, :, N - 1 : N]
+        parts, tails = [], []
+        for z in range(4):
+            q = slice(4 * s + z, 4 * s + z + 1)
+            part = (
+                g[:, z * N : (z + 1) * N]
+                + lam * from_before[q]
+                + mu * from_after[q]
+                + first * at_first[q]
+                + last * at_last[q]
+            )
+            g_out[s, z] = part
+            part = jnp.concatenate(
+                [part, col if z == 0 else pltpu.roll(col, N - 8 * z, 1)], axis=1
+            )
+            parts.append(part[0:N])
+            tails.append(part[N:EXT])
+        ends = dot3(hy[s], jnp.concatenate(parts + tails, axis=0), nt=True)
+        for p in range(6):
+            by_plane(pay, p, s, ends[p : p + 1, 0 : 4 * N])
+            pay[p, 16 + s : 17 + s, 0:32] = ends[p : p + 1, 4 * N : 4 * N + 32]
+    beside[0] = pay[4]
+    beside[1] = pay[5]
+    for m in range(ny):
+        send[m, 0:24] = pay[message(m, l)]
+        send[m, 24:48] = pay[4 + jnp.where(m > l, 1, 0)]
 
 
 def rows_kernel(nx, ny, f_in, recv, wx, gx, lx, hy, g_out, send, pay):
@@ -329,59 +442,64 @@
     for s in range(4):
         g = dot3(gx[s], f_in[s])
         lam, mu = lx[s, :, 0:1], lx[s, :, 1:2]
-        parts, tails = [], []
+        parts = []
         for z in range(4):
             q = 4 * s + z
             part = (
-                g[:, z * N : (z + 1) * N]
-                + lam * incoming[q : q + 1]
-                + mu * incoming[16 + q : 17 + q]
+                g[0:N, z * N : (z + 1) * N]
+                + lam[0:N] * incoming[q : q + 1]
+                + mu[0:N] * incoming[16 + q : 17 + q]
             )
             g_out[s, z] = part
-            parts.append(part[0:N])
-            tails.append(part[N:EXT])
-        ends = dot3(hy[s], jnp.concatenate(parts + tails, axis=0), nt=True)
+            parts.append(part)
+        ends = dot3(hy[s, :, 0:N], jnp.concatenate(parts, axis=0), nt=True)
         for p in range(2):
-            for z in range(4):
-                q = 4 * s + z
-                pay[p, q : q + 1, :] = ends[p : p + 1, z * N : (z + 1) * N]
-            pay[p, 16 + s : 17 + s, 0:32] = ends[p : p + 1, 4 * N : 4 * N + 32]
-    a, b = pay[0], pay[1]
+            by_plane(pay, p, s, ends[p : p + 1])
     for m in range(ny):
-        send[m] = jnp.where(m > l, a, b)
-
-
-def cols_part(ny, g_in, recv, wy, gy, ry, s, turned, wide):
-    width = 2 * N if wide else N
-    g = g_in[s].reshape(4 * EXT, N)
-    out = dot3(g, gy[s, :, 0:width])
-    lam, mu = ry[s, 0:1, 0:width], ry[s, 1:2, 0:width]
-    result = []
-    for z in range(4):
-        q = 4 * s + z
-
-        def column(p):
-            main = turned[:, 16 * p + q : 16 * p + q + 1]
-            tail = turned[8 * z : 8 * z + 8, 32 + 4 * p + s : 33 + 4 * p + s]
-            return jnp.concatenate([main, tail], axis=0)
-
-        result.append(
-            out[z * EXT : (z + 1) * EXT] + column(0) * lam + column(1) * mu
-        )
-    return result
-
-
-def turned_of(ny, recv, wy, turned):
-    incoming = dot3(wy[...], recv[...].reshape(ny * 24, N))
-    turned[...] = jnp.concatenate([incoming, jnp.zeros((N - 40, N), f32)], axis=0).T
-
-
-def next_kernel(nx, ny, g_in, recv, wy, gy, ry, rate, hx, kin, cross, f_out, send, st, turned, pay):
-    turned_of(ny, recv, wy, turned)
-    for s in range(4):
-        parts = cols_part(ny, g_in, recv, wy, gy, ry, s, turned, True)
+        send[m] = pay[(m < l).astype(jnp.int32)]
+
+
+def outer_sum(out, turned, pairs, q, s):
+    for main, tail, row in pairs:
+        col = turned[:, main + q : main + q + 1]
+        if tail is not None:
+            at = 8 * (q % 4)
+            col = jnp.concatenate(
+                [col, turned[at : at + 8, tail + s : tail + s + 1]], axis=0
+            )
+        out = out + col * row
+    return out
+
+
+def next_kernel(
+    nx, ny, g_in, recv, beside, wy, gy, ry, rate, hx, kin, cross, f_out, send, st, turned, pay
+):
+    l = lax.axis_index("col")
+    incoming = dot3(wy[...], recv[:, 0:24, :].reshape(ny * 24, N))
+    at_first = recv[jnp.maximum(l - 1, 0), 24:48, :] * (l > 0).astype(f32)
+    at_last = recv[jnp.minimum(l + 1, ny - 1), 24:48, :] * (l < ny - 1).astype(f32)
+    turned[...] = jnp.concatenate(
+        [
+            incoming[0:16] + beside[0, 0:16, :],
+            incoming[16:32] + beside[1, 0:16, :],
+            incoming[32:40] + beside[0, 16:24, :],
+            incoming[40:48] + beside[1, 16:24, :],
+            at_first,
+            at_last,
+            jnp.zeros((N - 96, N), f32),
+        ],
+        axis=0,
+    ).T
+    for s in range(4):
+        out = dot3(g_in[s].reshape(4 * EXT, N), gy[s])
+        pairs = [
+            (0, 32, ry[s, 0:1]),
+            (16, 40, ry[s, 1:2]),
+            (48, 64, gy[s, 0:1]),
+            (72, 88, gy[s, N - 1 : N]),
+        ]
         for z in range(4):
-            st[s, z] = parts[z]
+            st[s, z] = outer_sum(out[z * EXT : (z + 1) * EXT], turned, pairs, 4 * s + z, s)
 
     def halo_of(s, z):
         return (
@@ -397,11 +515,13 @@
 
 
 def last_kernel(ny, g_in, recv, wy, gy, ry, out, turned):
-    turned_of(ny, recv, wy, turned)
-    for s in range(4):
-        parts = cols_part(ny, g_in, recv, wy, gy, ry, s, turned, False)
+    incoming = dot3(wy[...], recv[...].reshape(ny * 16, N))
+    turned[...] = jnp.concatenate([incoming, jnp.zeros((N - 32, N), f32)], axis=0).T
+    for s in range(4):
+        res = dot3(g_in[s].reshape(4 * N, N), gy[s, :, 0:N])
+        pairs = [(0, None, ry[s, 0:1, 0:N]), (16, None, ry[s, 1:2, 0:N])]
         for z in range(4):
-            out[s, z] = parts[z][0:N]
+            out[s, z] = outer_sum(res[z * N : (z + 1) * N], turned, pairs, 4 * s + z, s)
 
 
 def call(body, outs, scratch, smem=0, cost=3_000_000):
@@ -427,41 +547,41 @@
 
 def on_device(adjoint, rate_scale, kinetics, cross_matrix, x_diffusion, y_diffusion):
     nx, ny = lax.axis_size("row"), lax.axis_size("col")
-    row_edges, col_edges = call(edges_kernel, [(2, 16, N), (2, 16, N)], [])(adjoint)
-    up = lax.ppermute(row_edges[1], "row", [(i, i + 1) for i in range(nx - 1)])
-    down = lax.ppermute(row_edges[0], "row", [(i + 1, i) for i in range(nx - 1)])
-    left = lax.ppermute(col_edges[1], "col", [(i, i + 1) for i in range(ny - 1)])
-    right = lax.ppermute(col_edges[0], "col", [(i + 1, i) for i in range(ny - 1)])
-    gx, lx, hx, gy, ry, hy, wx, wy = call(
-        functools.partial(tables_kernel, nx, ny),
+    part = functools.partial
+    gx, lx, hx, gy, ry, hy, wx, wx_cols, wy, wy_last = call(
+        part(tables_kernel, nx, ny),
         [
-            (4, EXT, N), (4, EXT, N), (4, 8, N), (4, N, 2 * N), (4, 8, 2 * N), (4, 8, N),
-            (32, nx * 16), (40, ny * 24),
+            (4, EXT, N), (4, EXT, N), (4, 8, N), (4, N, 2 * N), (4, 8, 2 * N), (4, 8, 2 * N),
+            (32, nx * 16), (16, nx * 8), (48, ny * 24), (32, ny * 16),
         ],
         [(N, N)] * 8,
     )(x_diffusion, y_diffusion)
-    f_shape, g_shape = (4, N, 4 * N), (4, 4, EXT, N)
-    send_x, send_y = (nx, 16, N), (ny, 24, N)
+    f_shape = (4, N, 4 * N)
+    f, send, cells, cols = call(
+        part(first_kernel, nx, ny),
+        [f_shape, (nx, 40, N), (2, 16, N), (4, N, N)],
+        [(4, 40, N)],
+        2,
+    )(adjoint, rate_scale, hx, kinetics, cross_matrix)
+    recv = lax.all_to_all(send, "row", 0, 0, tiled=True)
+    g, send, beside = call(
+        part(first_rows_kernel, nx, ny),
+        [(4, 4, EXT, N), (ny, 48, N), (2, 24, N)],
+        [(6, 24, N)],
+    )(f, cells, cols, recv, wx, wx_cols, gx, lx, hy)
+    recv = lax.all_to_all(send, "col", 0, 0, tiled=True)
     f, send = call(
-        functools.partial(first_kernel, nx), [f_shape, send_x], [(N, N), (2, 16, N)], 2
-    )(adjoint, rate_scale, up, down, left, right, hx, kinetics, cross_matrix)
-    for step in range(STEPS):
-        recv = lax.all_to_all(send, "row", 0, 0, tiled=True)
-        g, send = call(
-            functools.partial(rows_kernel, nx, ny), [g_shape, send_y], [(2, 24, N)]
-        )(f, recv, wx, gx, lx, hy)
-        recv = lax.all_to_all(send, "col", 0, 0, tiled=True)
-        if step + 1 < STEPS:
-            f, send = call(
-                functools.partial(next_kernel, nx, ny),
-                [f_shape, send_x],
-                [(4, 4, EXT, 2 * N), (N, N), (2, 16, N)],
-                2,
-            )(g, recv, wy, gy, ry, rate_scale, hx, kinetics, cross_matrix)
-        else:
-            (out,) = call(functools.partial(last_kernel, ny), [(4, 4, N, N)], [(N, N)])(
-                g, recv, wy, gy, ry
-            )
+        part(next_kernel, nx, ny),
+        [f_shape, (nx, 16, N)],
+        [(4, 4, EXT, 2 * N), (N, N), (2, 16, N)],
+        2,
+    )(g, recv, beside, wy, gy, ry, rate_scale, hx, kinetics, cross_matrix)
+    recv = lax.all_to_all(send, "row", 0, 0, tiled=True)
+    g, send = call(
+        part(rows_kernel, nx, ny), [(4, 4, N, N), (ny, 16, N)], [(2, 16, N)]
+    )(f, recv, wx, gx, lx, hy)
+    recv = lax.all_to_all(send, "col", 0, 0, tiled=True)
+    (out,) = call(part(last_kernel, ny), [(4, 4, N, N)], [(N, N)])(g, recv, wy_last, gy, ry)
     return out
 
 

time: 86.6 us -> 82.1 us (0.948)
  starting transfers between devices: 13 us -> 0 us
  blocking collectives: 56.2 us -> 62.6 us
  Pallas kernels: 15.5 us -> 17.4 us
    ppermute x4 -> x0, starting transfers between devices: 13 us -> none  [the longest x1 5 us: on_device(): lax.ppermute(col_edges[1], 'col', [(i, i + 1) for i in range(ny - 1)])]
    all_to_all x2, blocking collectives: 30.7 us -> 36.5 us  [on_device(): recv = lax.all_to_all(send, 'row', 0, 0, tiled=True)]
    pallas_call x7 -> x6, Pallas kernels: 15.5 us -> 17.4 us  [run(): pl.pallas_call(body, out_shape=shapes, in_specs=[pl.BlockSpec(memory_spac...]
  transfers between devices with their start and end apart: 4 -> 0, of which waited for: 0 -> 0; matrix products, arithmetic and copies ran while one was open for 0% -> 0% of each run, Pallas kernels for 3% -> 0%
where the time goes in v2:
time: 82.1 us; the launch traced here: 81.7 us
  blocking collectives  62.6 us (76%)
  Pallas kernels  17.4 us (21%)
  local copies, waits for them, and re-layouts  1.66 us (2%)
    all_to_all x2, blocking collectives, on_device(): recv = lax.all_to_all(send, 'row', 0, 0, tiled=True)  36.5 us
    all_to_all x2, blocking collectives, on_device(): recv = lax.all_to_all(send, 'col', 0, 0, tiled=True)  26.1 us
    pallas_call x6, Pallas kernels, run(): pl.pallas_call(body, out_shape=shapes, in_specs=[pl.BlockSpec(memory_spac...  17.4 us
    unnamed x12, local copies, waits for them, and re-layouts  1.66 us

profile of v2, /device:TPU:1, one launch (start us, length us, event | category | flops | bytes accessed | tf_op | source)
XLA Modules:
  0.0 81.7 jit_solution(16427990735932264265)
XLA Ops:
  0.0 0.0 copy-start.1
  0.0 0.0 copy-start.2
  0.0 0.9 %copy-done.2 = f32[4,4096]{1,0:T(4,128)S(1)} copy-done((f32[4,4096]{1,0:T(4,128)S(1)}, f32[4,4096]{1,0:T(4,128)}, u32[]{:S(2)}) %copy-start.2) | copy-done | bytes 65560
  0.9 0.0 copy-start.3
  0.9 0.7 copy-done.3
  1.6 0.0 copy-start
  1.7 0.0 copy-start.4
  1.7 0.0 copy-start.5
  1.7 3.3 %shard_map.64 = (f32[4,136,128]{2,1,0:T(8,128)S(1)}, f32[4,136,128]{2,1,0:T(8,128)S(1)}, f32[4,8,128]{2,1,0:T(8,128)S(1)}, f32[4,128,256]{2,1,0:T(8,128)S(1)}, f...) custom-call(f32[4,4096]{1,0:T(4,128)S(1)} %copy-done.2, ...), custom_call_target="tpu_custom_call" | custom-call | flops 3000000000 | bytes 3000000 | tf_op jit(solution)/shard_map/pallas_call | solution.py:532
  5.0 0.0 copy-done.1
  5.0 0.0 copy-done
  5.0 0.0 copy-done.4
  5.0 0.0 copy-done.5
  5.0 2.8 %shard_map.65 = (f32[4,128,512]{2,1,0:T(8,128)S(1)}, f32[32,40,128]{2,1,0:T(8,128)S(1)}, f32[2,16,128]{2,1,0:T(8,128)S(1)}, f32[4,128,128]{2,1,0:T(8,128)S(1)}) custom-call(f32[4,4,128,128]{3,2,1,0:T(8,128)S(1)} %copy-done, f32[4,4,128,128]{3,2,1,0:T(8,128)S(1)} %copy-done.1, f32[4,8,128]{2,1,0:T(8,128)S(1)} %get-tuple-element.26.hx, f32[4,4]{1,0:T(4,128)S(1)} %copy-done.4, ...), custom_call_target="tpu_custom_call" | custom-call | flops 3000000000 | bytes 3000000 | tf_op jit(solution)/shard_map/pallas_call | solution.py:532
  7.8 21.3 %all_to_all.20.recv = f32[32,40,128]{2,1,0:T(8,128)S(1)} all-to-all(f32[32,40,128]{2,1,0:T(8,128)S(1)} %get-tuple-element.30), channel_id=1, replica_groups=mesh['row'=32,'col'=8] {'row'}, dimensions={0} | all-to-all | bytes 1310720 | tf_op jit(solution)/shard_map/all_to_all | solution.py:566
  29.1 2.5 %shard_map.66 = (f32[4,4,136,128]{3,2,1,0:T(8,128)S(1)}, f32[8,48,128]{2,1,0:T(8,128)S(1)}, f32[2,24,128]{2,1,0:T(8,128)S(1)}) custom-call(f32[4,128,512]{2,1,0:T(8,128)S(1)} %get-tuple-element.27.f_in, f32[2,16,128]{2,1,0:T(8,128)S(1)} %get-tuple-element.28.cells, f32[4,128,128]{2,1,0:T(8,128)S(1)} %get-tuple-element.29.cols, ...), custom_call_target="tpu_custom_call" | custom-call | flops 3000000000 | bytes 3000000 | tf_op jit(solution)/shard_map/pallas_call | solution.py:532
  31.7 16.6 %all_to_all.21.recv = f32[8,48,128]{2,1,0:T(8,128)S(1)} all-to-all(f32[8,48,128]{2,1,0:T(8,128)S(1)} %get-tuple-element.37), channel_id=1, replica_groups=mesh['row'=32,'col'=8] {'col'}, dimensions={0} | all-to-all | bytes 393216 | tf_op jit(solution)/shard_map/all_to_all | solution.py:572
  48.3 5.2 %shard_map.67 = (f32[4,128,512]{2,1,0:T(8,128)S(1)}, f32[32,16,128]{2,1,0:T(8,128)S(1)}) custom-call(f32[4,4,136,128]{3,2,1,0:T(8,128)S(1)} %get-tuple-element.36.g_in, f32[8,48,128]{2,1,0:T(8,128)S(1)} %all_to_all.21.recv, f32[2,24,128]{2,1,0:T(8,128)S(1)} %get-tuple-element.38.beside, f32[48,192]{1,0:T(8,128)S(1)} %get-tuple-element.39.wy, ...), custom_call_target="tpu_custom_call" | custom-call | flops 3000000000 | bytes 3000000 | tf_op jit(solution)/shard_map/pallas_call | solution.py:532
  53.5 15.2 %all_to_all.22.recv = f32[32,16,128]{2,1,0:T(8,128)S(1)} all-to-all(f32[32,16,128]{2,1,0:T(8,128)S(1)} %get-tuple-element.43), channel_id=1, replica_groups=mesh['row'=32,'col'=8] {'row'}, dimensions={0} | all-to-all | bytes 524288 | tf_op jit(solution)/shard_map/all_to_all | solution.py:579
  68.7 1.5 %shard_map.68 = (f32[4,4,128,128]{3,2,1,0:T(8,128)S(1)}, f32[8,16,128]{2,1,0:T(8,128)S(1)}) custom-call(f32[4,128,512]{2,1,0:T(8,128)S(1)} %get-tuple-element.42.f_in, f32[32,16,128]{2,1,0:T(8,128)S(1)} %all_to_all.22.recv, f32[32,512]{1,0:T(8,128)S(1)} %get-tuple-element.31.wx, f32[4,136,128]{2,1,0:T(8,128)S(1)} %get-tuple-element.33.gx, ...), custom_call_target="tpu_custom_call" | custom-call | flops 3000000000 | bytes 3000000 | tf_op jit(solution)/shard_map/pallas_call | solution.py:532
  70.2 9.5 %all_to_all.23.recv = f32[8,16,128]{2,1,0:T(8,128)S(1)} all-to-all(f32[8,16,128]{2,1,0:T(8,128)S(1)} %get-tuple-element.45), channel_id=1, replica_groups=mesh['row'=32,'col'=8] {'col'}, dimensions={0} | all-to-all | bytes 131072 | tf_op jit(solution)/shard_map/all_to_all | solution.py:583
  79.7 2.0 %shard_map.69 = f32[4,4,128,128]{3,2,1,0:T(8,128)} custom-call(f32[4,4,128,128]{3,2,1,0:T(8,128)S(1)} %get-tuple-element.44.g_in, f32[8,16,128]{2,1,0:T(8,128)S(1)} %all_to_all.23.recv, f32[32,128]{1,0:T(8,128)S(1)} %get-tuple-element.46.wy, f32[4,128,256]{2,1,0:T(8,128)S(1)} %get-tuple-element.40.gy, f32[4,8,256]{2,1,0:T(8,128)S(1)} %get-tuple-element.41.ry), custom_call_target="tpu_custom_call" | custom-call | flops 3000000000 | bytes 3000000 | tf_op jit(solution)/shard_map/pallas_call | solution.py:532
Async XLA Ops:
  0.0 5.0 %copy-start.1 = (f32[4,4,128,128]{3,2,1,0:T(8,128)S(1)}, f32[4,4,128,128]{3,2,1,0:T(8,128)}, u32[]{:S(2)}) copy-start(f32[4,4,128,128]{3,2,1,0:T(8,128)} %rate.3) | copy-start | bytes 3145732
  0.0 0.9 %copy-start.2 = (f32[4,4096]{1,0:T(4,128)S(1)}, f32[4,4096]{1,0:T(4,128)}, u32[]{:S(2)}) copy-start(f32[4,4096]{1,0:T(4,128)} %xd.1) | copy-start | bytes 196612
  0.9 0.7 copy-start.3
  1.6 3.3 %copy-start = (f32[4,4,128,128]{3,2,1,0:T(8,128)S(1)}, f32[4,4,128,128]{3,2,1,0:T(8,128)}, u32[]{:S(2)}) copy-start(f32[4,4,128,128]{3,2,1,0:T(8,128)} %state.1) | copy-start | bytes 3145732
  1.7 3.3 %copy-start.4 = (f32[4,4]{1,0:T(4,128)S(1)}, f32[4,4]{1,0:T(4,128)}, u32[]{:S(2)}) copy-start(f32[4,4]{1,0:T(4,128)} %kin.3) | copy-start | bytes 196
  1.7 3.3 %copy-start.5 = (f32[4,4]{1,0:T(4,128)S(1)}, f32[4,4]{1,0:T(4,128)}, u32[]{:S(2)}) copy-start(f32[4,4]{1,0:T(4,128)} %cross.3) | copy-start | bytes 196

commit v3 on v2

v3 whole, which is shorter than its diff:
```python
import functools

import jax
import jax.numpy as jnp
from jax import lax
from jax.experimental import pallas as pl
from jax.experimental.pallas import tpu as pltpu
from jax.sharding import PartitionSpec as P

M = 1000.0
STEPS = 2
N = 128
f32 = jnp.float32
bf16 = jnp.bfloat16
VMEM = 20 * 1024 * 1024


def iota(shape, dim):
    return lax.broadcasted_iota(jnp.int32, shape, dim)


def split(a):
    hi = a.astype(bf16)
    return hi, (a - hi.astype(f32)).astype(bf16)


def dot3(a, b, nt=False):
    dims = (((1,), (1 if nt else 0,)), ((), ()))
    ah, al = split(a)
    bh, bl = split(b)

    def dot(p, q):
        return lax.dot_general(p, q, dims, preferred_element_type=f32)

    return dot(ah, bh) + (dot(ah, bl) + dot(al, bh))


def tables_kernel(
    nx, ny, xd_in, yd_in, gx, lx, hx, gy, ry, hy, wx, wx_cols, wy,
    rows_x, rows_y, ex, ey, p0, p1, q0, q1, xd, yd, arrived,
):
    k = lax.axis_index("row")
    l = lax.axis_index("col")
    scale = 1.0 / M
    x_copy = pltpu.make_async_copy(xd_in, xd, arrived.at[0])
    y_copy = pltpu.make_async_copy(yd_in, yd, arrived.at[1])
    x_copy.start()
    y_copy.start()
    rows_x[...] = jnp.full((N, N), scale, f32)
    rows_y[...] = jnp.full((N, N), scale, f32)
    x_copy.wait()
    y_copy.wait()
    for j in range(nx):
        rows_x[4 * j : 4 * j + 4, :] = scale / xd[:, j * N : (j + 1) * N]
    for j in range(ny):
        rows_y[4 * j : 4 * j + 4, :] = scale / yd[:, j * N : (j + 1) * N]

    def block(ref, index):
        return scale / ref[:, pl.ds(pl.multiple_of(index * N, N), N)]

    rows_y[32:36, :] = block(xd, k)
    rows_y[36:40, :] = block(yd, l)
    ex[...] = rows_x[...].T
    ey[...] = rows_y[...].T

    first2 = (iota((2, N), 0) == 0).astype(f32)
    one, zero = jnp.ones((1, N), f32), jnp.zeros((1, N), f32)

    def body(i, carry):
        vx, dx, va, da, vb, db, ux, cx, ua, ca, ub, cb = carry
        at = pl.multiple_of(i * 8, 8)
        back = pl.multiple_of(N - 8 - i * 8, 8)
        ex_f, ey_f = ex[pl.ds(at, 8), :], ey[pl.ds(at, 8), :]
        ex_b, ey_b = ex[pl.ds(back, 8), :], ey[pl.ds(back, 8), :]
        for r in range(8):
            t = at + r
            p0[pl.ds(t, 1), :] = va
            p1[pl.ds(t, 1), :] = vb
            e, ee = ex_f[r : r + 1], ey_f[r : r + 1]
            dx = dx + e * vx
            vx = vx + dx
            da = da + ee * va
            va = va + da
            db = db + ee * vb
            vb = vb + db
            r2 = 7 - r
            t = back + r2
            q0[pl.ds(t, 1), :] = ua
            q1[pl.ds(t, 1), :] = ub
            e, ee = ex_b[r2 : r2 + 1], ey_b[r2 : r2 + 1]
            cx = cx + e * ux
            ux = ux + cx
            ca = ca + ee * ua
            ua = ua + ca
            cb = cb + ee * ub
            ub = ub + cb
        return vx, dx, va, da, vb, db, ux, cx, ua, ca, ub, cb

    init = (first2, 1.0 - first2, one, zero, zero, one)
    vx, dx, va, da, vb, db, ux, cx, ua, ca, ub, cb = lax.fori_loop(
        0, N // 8, body, init + init
    )

    row = iota((8, N), 0)
    lane = iota((8, N), 1)
    blk = lane // 4
    forward = row < 2
    is_x = row % 2 == 0
    count = jnp.where(is_x, nx, ny)
    own = jnp.where(is_x, k, l)
    place = jnp.where(forward, blk, count - 1 - blk)
    own = jnp.where(forward, own, count - 1 - own)

    def pack(a, b, c, d):
        return jnp.where(
            row == 0, a, jnp.where(row == 1, b, jnp.where(row == 2, c, d))
        )

    def shifted(a, by):
        return jnp.where(
            forward, pltpu.roll(a, 4 * by, 1), pltpu.roll(a, N - 4 * by, 1)
        )

    def outside(by):
        return place < by

    a0 = pack(vx[0:1], va, ux[0:1], ua)
    b0 = pack(vx[1:2], vb, ux[1:2], ub)
    c0 = pack(dx[0:1], da, cx[0:1], ca)
    d0 = pack(dx[1:2], db, cx[1:2], cb)
    a, b, c, d = a0, b0, c0, d0
    by = 1
    while by < max(nx, ny):
        skip = outside(by)
        sa = jnp.where(skip, 1.0, shifted(a, by))
        sb = jnp.where(skip, 0.0, shifted(b, by))
        sc = jnp.where(skip, 0.0, shifted(c, by))
        sd = jnp.where(skip, 1.0, shifted(d, by))
        a, b, c, d = a * sa + b * sc, a * sb + b * sd, c * sa + d * sc, c * sb + d * sd
        norm = 1.0 / (a + b)
        a, b, c, d = a * norm, b * norm, c * norm, d * norm
        by *= 2
    skip = outside(1)
    slope = jnp.where(skip, 1.0, shifted((c + d) / (a + b), 1))

    decay = (1.0 - slope) / ((a0 + b0 * slope) - (c0 + d0 * slope))
    between = (place < own) & (place >= 0)
    prod = jnp.where(between, decay, 1.0)

    def against(a, by):
        return jnp.where(
            forward, pltpu.roll(a, N - 4 * by, 1), pltpu.roll(a, 4 * by, 1)
        )

    def past(by):
        return place + by >= count

    by = 1
    while by < max(nx, ny):
        prod = prod * jnp.where(past(by), 1.0, against(prod, by))
        by *= 2
    weight = jnp.where(between, jnp.where(past(1), 1.0, against(prod, 1)), 0.0)

    def expand(width, per_block, species_of):
        src = iota((N, width), 0)
        col = iota((N, width), 1)
        hit = (src // 4 == col // per_block) & (src % 4 == species_of(col % per_block))
        return lax.dot_general(
            weight,
            jnp.where(hit, 1.0, 0.0),
            (((1,), (0,)), ((), ())),
            precision=lax.Precision.HIGHEST,
            preferred_element_type=f32,
        )

    width = nx * 16
    spread = expand(width, 16, lambda r: r // 4)
    rr, cc = iota((32, width), 0), iota((32, width), 1)
    wx[...] = jnp.where(
        rr % 16 == cc % 16, jnp.where(rr < 16, spread[0:1], spread[2:3]), 0.0
    )
    width = nx * 8
    spread = expand(width, 8, lambda r: r)
    rr, cc = iota((16, width), 0), iota((16, width), 1)
    wx_cols[...] = jnp.where(
        rr % 8 == cc % 8, jnp.where(rr < 8, spread[0:1], spread[2:3]), 0.0
    )
    width = ny * 16
    spread = expand(width, 16, lambda r: r // 4)
    rr, cc = iota((32, width), 0), iota((32, width), 1)
    wy[...] = jnp.where(
        rr % 16 == cc % 16, jnp.where(rr < 16, spread[1:2], spread[3:4]), 0.0
    )

    lane1 = iota((1, N), 1)
    to_x = lax.rem(32 - 4 * k + N, N)
    to_y = lax.rem(36 - 4 * l + N, N)
    sx = pltpu.roll(slope, to_x, 1)
    sy = pltpu.roll(slope, to_y, 1)
    valid = (lane1 >= 32) & (lane1 < 40)
    sf = jnp.where(valid, jnp.where(lane1 < 36, sx[0:1], sy[1:2]), 1.0)
    sb = jnp.where(valid, jnp.where(lane1 < 36, sx[2:3], sy[3:4]), 1.0)
    phi = p0[...] + p1[...] * sf
    psi = q0[...] + q1[...] * sb
    phi_before, phi_after = 1.0 - sf, va + vb * sf
    psi_after, psi_before = 1.0 - sb, ua + ub * sb
    wron = sf * psi_before + (ca + cb * sb) * phi_before
    inv_w = 1.0 / wron
    psi = psi * inv_w
    psi_after, psi_before = psi_after * inv_w, psi_before * inv_w
    phi_t, psi_t = phi.T, psi.T
    eps = ey[...]
    eps_t = rows_y[...]
    i0, j0 = iota((N, N), 0), iota((N, N), 1)
    low = i0 >= j0
    r8 = iota((8, N), 0)
    c8 = iota((8, N), 1)
    for s in range(4):
        at = slice(32 + s, 33 + s)
        pr, qr = phi_t[at], psi_t[at]
        pc, qc, ec = phi[:, at], psi[:, at], eps[:, at]
        pb, pa, qb, qa = phi_before[:, at], phi_after[:, at], psi_before[:, at], psi_after[:, at]
        eq, ep = ec * qc, ec * pc
        gx[s] = jnp.where(low, eq * pr, ep * qr)
        lx[s] = jnp.where(j0 == 0, eq * pb, jnp.where(j0 == 1, ep * qa, 0.0))
        inv_p, inv_q = 1.0 / pr[:, N - 1 : N], 1.0 / qr[:, 0:1]
        beside = jnp.where(
            c8 == 0,
            pb * inv_p,
            jnp.where(c8 == 1, pa * inv_p, jnp.where(c8 == 2, qb * inv_q, qa * inv_q)),
        )
        hx[s] = jnp.where(
            r8 == 0,
            pr * inv_p,
            jnp.where(r8 == 1, qr * inv_q, jnp.where(r8 == 2, beside, 0.0)),
        )

        at = slice(36 + s, 37 + s)
        pr, qr, er = phi_t[at], psi_t[at], eps_t[at]
        pc, qc = phi[:, at], psi[:, at]
        pb, pa, qb, qa = phi_before[:, at], phi_after[:, at], psi_before[:, at], psi_after[:, at]
        gy[s] = jnp.where(low, qc * (pr * er), pc * (qr * er))
        ry[s] = jnp.where(r8 == 0, pb * qr * er, jnp.where(r8 == 1, qa * pr * er, 0.0))
        inv_p, inv_q = 1.0 / pr[:, N - 1 : N], 1.0 / qr[:, 0:1]
        hy[s, :, 0:N] = jnp.where(
            r8 == 0, pr * inv_p, jnp.where(r8 == 1, qr * inv_q, 0.0)
        )
        before = jnp.where(
            r8 == 0, pb * inv_p, jnp.where(r8 == 1, qb * inv_q, jnp.where(r8 == 2, 1.0, 0.0))
        )
        after = jnp.where(
            r8 == 0, pa * inv_p, jnp.where(r8 == 1, qa * inv_q, jnp.where(r8 == 3, 1.0, 0.0))
        )
        hy[s, :, N:] = jnp.where(c8 == 0, before, jnp.where(c8 == 1, after, 0.0))


def by_plane(ref, p, s, values):
    for z in range(4):
        q = 4 * s + z
        ref[p, q : q + 1, :] = values[:, z * N : (z + 1) * N]


def explicit(nx, ny, state, rate, hx, kin, cross, f_out, send, cells, cols, pay):
    k, l = lax.axis_index("row"), lax.axis_index("col")
    i0, j0 = iota((N, N), 0), iota((N, N), 1)
    for z in range(4):
        tiles, laps = [], []
        for s in range(4):
            t = state[s, z]
            xm = jnp.where(i0 == 0, 0.0, pltpu.roll(t, 1, 0))
            xp = jnp.where(i0 == N - 1, 0.0, pltpu.roll(t, N - 1, 0))
            ym = jnp.where(j0 == 0, 0.0, pltpu.roll(t, 1, 1))
            yp = jnp.where(j0 == N - 1, 0.0, pltpu.roll(t, N - 1, 1))
            tiles.append(t)
            laps.append(xm + xp + ym + yp - 4.0 * t)
        for j in range(4):
            react = kin[0, j] * tiles[0]
            mix = cross[0, j] * laps[0]
            for i in range(1, 4):
                react = react + kin[i, j] * tiles[i]
                mix = mix + cross[i, j] * laps[i]
            f_out[j, :, z * N : (z + 1) * N] = (
                tiles[j] + 0.5 * rate[j, z] * react + 0.25 * mix
            )

    side = []
    for s in range(4):
        acc = jnp.zeros((N, N), f32)
        for z in range(4):
            tile = state[s, z]
            acc = jnp.where(j0 == 8 * z, tile[:, 0:1], acc)
            acc = jnp.where(j0 == 8 * z + 1, tile[:, N - 1 : N], acc)
        side.append(acc)
    has = jnp.where(j0 % 8 == 0, (l > 0).astype(f32), (l < ny - 1).astype(f32))
    has_x = 0.25 * (k > 0).astype(f32), 0.25 * (k < nx - 1).astype(f32)
    pay[...] = jnp.zeros_like(pay)
    for j in range(4):
        mix = cross[0, j] * side[0]
        for i in range(1, 4):
            mix = mix + cross[i, j] * side[i]
        mix = 0.25 * has * mix
        cols[j] = mix
        beside = []
        for p, row in enumerate((0, N - 1)):
            pieces = []
            for z in range(4):
                piece = cross[0, j] * state[0, z, row : row + 1, :]
                for i in range(1, 4):
                    piece = piece + cross[i, j] * state[i, z, row : row + 1, :]
                pieces.append(has_x[p] * piece)
            beside.append(jnp.concatenate(pieces, axis=1))
            by_plane(cells, p, j, beside[p])
        sums = dot3(hx[j], f_out[j])
        ends = dot3(hx[j], mix)
        for p in range(2):
            c = hx[j, 2:3, 2 * p : 2 * p + 1], hx[j, 2:3, 2 * p + 1 : 2 * p + 2]
            by_plane(pay, p, j, sums[p : p + 1] + c[0] * beside[0] + c[1] * beside[1])
            pay[p, 16 + j : 17 + j, :] = ends[p : p + 1]
    for j in range(nx):
        send[j] = pay[(j < k).astype(jnp.int32)]


def rows_kernel(
    nx, ny, f_in, cells, cols, recv, wx, wx_cols, gx, lx, hy, g_out, send, beside, pay
):
    l = lax.axis_index("col")
    incoming = dot3(wx[...], recv[:, 0:16, :].reshape(nx * 16, N))
    in_cols = dot3(wx_cols[...], recv[:, 16:24, :].reshape(nx * 8, N))
    from_before = incoming[0:16] + cells[0]
    from_after = incoming[16:32] + cells[1]
    for s in range(4):
        g = dot3(gx[s], f_in[s])
        lam, mu = lx[s, :, 0:1], lx[s, :, 1:2]
        col = (
            dot3(gx[s], cols[s])
            + lam * in_cols[s : s + 1]
            + mu * in_cols[8 + s : 9 + s]
        )
        parts = []
        for z in range(4):
            q = slice(4 * s + z, 4 * s + z + 1)
            part = (
                g[:, z * N : (z + 1) * N] + lam * from_before[q] + mu * from_after[q]
            )
            g_out[s, z] = part
            edge = col if z == 0 else pltpu.roll(col, N - 8 * z, 1)
            parts.append(jnp.concatenate([part, edge], axis=1))
        ends = dot3(hy[s], jnp.concatenate(parts, axis=0), nt=True)
        for p in range(2):
            by_plane(pay, p, s, ends[p : p + 1])
            by_plane(beside, p, s, ends[2 + p : 3 + p])
    for m in range(ny):
        send[m] = pay[(m < l).astype(jnp.int32)]


def finish_cols(ny, g_in, recv, beside, wy, gy, ry, out, turned):
    incoming = dot3(wy[...], recv[...].reshape(ny * 16, N))
    turned[...] = jnp.concatenate(
        [
            incoming[0:16] + beside[0],
            incoming[16:32] + beside[1],
            jnp.zeros((N - 32, N), f32),
        ],
        axis=0,
    ).T
    for s in range(4):
        res = dot3(g_in[s].reshape(4 * N, N), gy[s])
        lam, mu = ry[s, 0:1], ry[s, 1:2]
        for z in range(4):
            q = 4 * s + z
            out[s, z] = (
                res[z * N : (z + 1) * N]
                + turned[:, q : q + 1] * lam
                + turned[:, 16 + q : 17 + q] * mu
            )


def next_kernel(
    nx, ny, g_in, recv, beside, wy, gy, ry, rate, hx, kin, cross,
    f_out, send, cells, cols, state, turned, pay,
):
    finish_cols(ny, g_in, recv, beside, wy, gy, ry, state, turned)
    explicit(nx, ny, state, rate, hx, kin, cross, f_out, send, cells, cols, pay)


def call(body, outs, scratch, smem=0, place=pltpu.VMEM):
    shapes = [jax.ShapeDtypeStruct(shape, f32) for shape in outs]

    def run(*args):
        count = len(args) - smem
        return pl.pallas_call(
            body,
            out_shape=shapes,
            in_specs=[pl.BlockSpec(memory_space=place)] * count
            + [pl.BlockSpec(memory_space=pltpu.SMEM)] * smem,
            out_specs=[pl.BlockSpec(memory_space=pltpu.VMEM)] * len(shapes),
            scratch_shapes=[
                pltpu.VMEM(shape, f32) if isinstance(shape, tuple) else shape
                for shape in scratch
            ],
            compiler_params=pltpu.CompilerParams(vmem_limit_bytes=VMEM),
            cost_estimate=pl.CostEstimate(
                flops=3_000_000_000, bytes_accessed=3_000_000, transcendentals=0
            ),
        )(*args)

    return run


def on_device(adjoint, rate_scale, kinetics, cross_matrix, x_diffusion, y_diffusion):
    nx, ny = lax.axis_size("row"), lax.axis_size("col")
    part = functools.partial
    gx, lx, hx, gy, ry, hy, wx, wx_cols, wy = call(
        part(tables_kernel, nx, ny),
        [
            (4, N, N), (4, N, N), (4, 8, N), (4, N, N), (4, 8, N), (4, 8, 2 * N),
            (32, nx * 16), (16, nx * 8), (32, ny * 16),
        ],
        [(N, N)] * 8 + [x_diffusion.shape, y_diffusion.shape, pltpu.SemaphoreType.DMA((2,))],
        place=pl.ANY,
    )(x_diffusion, y_diffusion)
    tile = (4, 4, N, N)
    step_out = [(4, N, 4 * N), (nx, 24, N), (2, 16, N), (4, N, N)]
    f, send, cells, cols = call(part(explicit, nx, ny), step_out, [(2, 24, N)], 2)(
        adjoint, rate_scale, hx, kinetics, cross_matrix
    )
    for step in range(STEPS):
        recv = lax.all_to_all(send, "row", 0, 0, tiled=True)
        g, send, beside = call(
            part(rows_kernel, nx, ny), [tile, (ny, 16, N), (2, 16, N)], [(2, 16, N)]
        )(f, cells, cols, recv, wx, wx_cols, gx, lx, hy)
        recv = lax.all_to_all(send, "col", 0, 0, tiled=True)
        if step + 1 < STEPS:
            f, send, cells, cols = call(
                part(next_kernel, nx, ny), step_out, [tile, (N, N), (2, 24, N)], 2
            )(g, recv, beside, wy, gy, ry, rate_scale, hx, kinetics, cross_matrix)
    (out,) = call(part(finish_cols, ny), [tile], [(N, N)])(g, recv, beside, wy, gy, ry)
    return out


def solution(mesh):
    return jax.shard_map(
        on_device,
        mesh=mesh,
        in_specs=(P(None, None, "row", "col"), P(None, None, "row", "col"), P(), P(), P(), P()),
        out_specs=P(None, None, "row", "col"),
        check_vma=False,
    )
```

time: 82.1 us -> 76.4 us (0.931)
  blocking collectives: 62.6 us -> 58.5 us
  Pallas kernels: 17.4 us -> 15.8 us
    all_to_all x2, blocking collectives: 36.5 us -> 33.7 us  [on_device(): recv = lax.all_to_all(send, 'row', 0, 0, tiled=True)]
    pallas_call x6, Pallas kernels: 17.4 us -> 15.8 us  [run(): pl.pallas_call(body, out_shape=shapes, in_specs=[pl.BlockSpec(memory_spac...]
    all_to_all x2, blocking collectives: 26.1 us -> 24.8 us  [on_device(): recv = lax.all_to_all(send, 'col', 0, 0, tiled=True)]
where the time goes in v3:
time: 76.4 us; the launch traced here: 76.1 us
  blocking collectives  58.5 us (77%)
  Pallas kernels  15.8 us (21%)
  local copies, waits for them, and re-layouts  1.66 us (2%)
    all_to_all x2, blocking collectives, on_device(): recv = lax.all_to_all(send, 'row', 0, 0, tiled=True)  33.7 us
    all_to_all x2, blocking collectives, on_device(): recv = lax.all_to_all(send, 'col', 0, 0, tiled=True)  24.8 us
    pallas_call x6, Pallas kernels, run(): pl.pallas_call(body, out_shape=shapes, in_specs=[pl.BlockSpec(memory_spac...  15.8 us
    unnamed x12, local copies, waits for them, and re-layouts  1.66 us

profile of v3, /device:TPU:1, one launch (start us, length us, event | category | flops | bytes accessed | tf_op | source)
XLA Modules:
  0.0 76.1 jit_solution(3242765980472204820)
XLA Ops:
  0.0 0.0 copy-start.1
  0.0 0.0 copy-start.2
  0.0 0.9 %copy-done.2 = f32[4,4096]{1,0:T(4,128)S(1)} copy-done((f32[4,4096]{1,0:T(4,128)S(1)}, f32[4,4096]{1,0:T(4,128)}, u32[]{:S(2)}) %copy-start.2) | copy-done | bytes 65560
  0.9 0.0 copy-start.3
  0.9 0.7 copy-done.3
  1.6 0.0 copy-start
  1.7 0.0 copy-start.4
  1.7 0.0 copy-start.5
  1.7 2.8 %shard_map.64 = (f32[4,128,128]{2,1,0:T(8,128)S(1)}, f32[4,128,128]{2,1,0:T(8,128)S(1)}, f32[4,8,128]{2,1,0:T(8,128)S(1)}, f32[4,128,128]{2,1,0:T(8,128)S(1)}, f...) custom-call(f32[4,4096]{1,0:T(4,128)S(1)} %copy-done.2, ...), custom_call_target="tpu_custom_call" | custom-call | flops 3000000000 | bytes 3000000 | tf_op jit(solution)/shard_map/pallas_call | solution.py:391
  4.5 0.0 copy-done.1
  4.5 0.0 copy-done
  4.5 0.0 copy-done.4
  4.5 0.0 copy-done.5
  4.5 2.8 %shard_map.65 = (f32[4,128,512]{2,1,0:T(8,128)S(1)}, f32[32,24,128]{2,1,0:T(8,128)S(1)}, f32[2,16,128]{2,1,0:T(8,128)S(1)}, f32[4,128,128]{2,1,0:T(8,128)S(1)}) custom-call(f32[4,4,128,128]{3,2,1,0:T(8,128)S(1)} %copy-done, f32[4,4,128,128]{3,2,1,0:T(8,128)S(1)} %copy-done.1, f32[4,8,128]{2,1,0:T(8,128)S(1)} %get-tuple-element.28.hx, f32[4,4]{1,0:T(4,128)S(1)} %copy-done.4, ...), custom_call_target="tpu_custom_call" | custom-call | flops 3000000000 | bytes 3000000 | tf_op jit(solution)/shard_map/pallas_call | solution.py:391
  7.3 18.6 %all_to_all.20.recv = f32[32,24,128]{2,1,0:T(8,128)S(1)} all-to-all(f32[32,24,128]{2,1,0:T(8,128)S(1)} %get-tuple-element.32), channel_id=1, replica_groups=mesh['row'=32,'col'=8] {'row'}, dimensions={0} | all-to-all | bytes 786432 | tf_op jit(solution)/shard_map/all_to_all | solution.py:428
  25.9 2.3 %shard_map.66 = (f32[4,4,128,128]{3,2,1,0:T(8,128)S(1)}, f32[8,16,128]{2,1,0:T(8,128)S(1)}, f32[2,16,128]{2,1,0:T(8,128)S(1)}) custom-call(f32[4,128,512]{2,1,0:T(8,128)S(1)} %get-tuple-element.29.f_in, f32[2,16,128]{2,1,0:T(8,128)S(1)} %get-tuple-element.30.cells, f32[4,128,128]{2,1,0:T(8,128)S(1)} %get-tuple-element.31.cols, ...), custom_call_target="tpu_custom_call" | custom-call | flops 3000000000 | bytes 3000000 | tf_op jit(solution)/shard_map/pallas_call | solution.py:391
  28.2 15.2 %all_to_all.21.recv = f32[8,16,128]{2,1,0:T(8,128)S(1)} all-to-all(f32[8,16,128]{2,1,0:T(8,128)S(1)} %get-tuple-element.39), channel_id=1, replica_groups=mesh['row'=32,'col'=8] {'col'}, dimensions={0} | all-to-all | bytes 131072 | tf_op jit(solution)/shard_map/all_to_all | solution.py:432
  43.4 3.6 %shard_map.67 = (f32[4,128,512]{2,1,0:T(8,128)S(1)}, f32[32,24,128]{2,1,0:T(8,128)S(1)}, f32[2,16,128]{2,1,0:T(8,128)S(1)}, f32[4,128,128]{2,1,0:T(8,128)S(1)}) custom-call(f32[4,4,128,128]{3,2,1,0:T(8,128)S(1)} %get-tuple-element.38.g_in, f32[8,16,128]{2,1,0:T(8,128)S(1)} %all_to_all.21.recv, f32[2,16,128]{2,1,0:T(8,128)S(1)} %get-tuple-element.40.beside, ...), custom_call_target="tpu_custom_call" | custom-call | flops 3000000000 | bytes 3000000 | tf_op jit(solution)/shard_map/pallas_call | solution.py:391
  47.1 15.2 %all_to_all.22.recv = f32[32,24,128]{2,1,0:T(8,128)S(1)} all-to-all(f32[32,24,128]{2,1,0:T(8,128)S(1)} %get-tuple-element.47), channel_id=1, replica_groups=mesh['row'=32,'col'=8] {'row'}, dimensions={0} | all-to-all | bytes 786432 | tf_op jit(solution)/shard_map/all_to_all | solution.py:428
  62.2 2.3 %shard_map.68 = (f32[4,4,128,128]{3,2,1,0:T(8,128)S(1)}, f32[8,16,128]{2,1,0:T(8,128)S(1)}, f32[2,16,128]{2,1,0:T(8,128)S(1)}) custom-call(f32[4,128,512]{2,1,0:T(8,128)S(1)} %get-tuple-element.44.f_in, f32[2,16,128]{2,1,0:T(8,128)S(1)} %get-tuple-element.45.cells, f32[4,128,128]{2,1,0:T(8,128)S(1)} %get-tuple-element.46.cols, ...), custom_call_target="tpu_custom_call" | custom-call | flops 3000000000 | bytes 3000000 | tf_op jit(solution)/shard_map/pallas_call | solution.py:391
  64.5 9.5 %all_to_all.23.recv = f32[8,16,128]{2,1,0:T(8,128)S(1)} all-to-all(f32[8,16,128]{2,1,0:T(8,128)S(1)} %get-tuple-element.49), channel_id=1, replica_groups=mesh['row'=32,'col'=8] {'col'}, dimensions={0} | all-to-all | bytes 131072 | tf_op jit(solution)/shard_map/all_to_all | solution.py:432
  74.1 2.0 %shard_map.69 = f32[4,4,128,128]{3,2,1,0:T(8,128)} custom-call(f32[4,4,128,128]{3,2,1,0:T(8,128)S(1)} %get-tuple-element.48.g_in, f32[8,16,128]{2,1,0:T(8,128)S(1)} %all_to_all.23.recv, f32[2,16,128]{2,1,0:T(8,128)S(1)} %get-tuple-element.50.beside, f32[32,128]{1,0:T(8,128)S(1)} %get-tuple-element.41.wy, f32[4,128,128]{2,1,0:T(8,128)S(1)} %get-tuple-element.42.gy, ...), custom_call_target="tpu_custom_call" | custom-call | flops 3000000000 | bytes 3000000 | tf_op jit(solution)/shard_map/pallas_call | solution.py:391
Async XLA Ops:
  0.0 4.5 %copy-start.1 = (f32[4,4,128,128]{3,2,1,0:T(8,128)S(1)}, f32[4,4,128,128]{3,2,1,0:T(8,128)}, u32[]{:S(2)}) copy-start(f32[4,4,128,128]{3,2,1,0:T(8,128)} %rate.3) | copy-start | bytes 3145732
  0.0 0.9 %copy-start.2 = (f32[4,4096]{1,0:T(4,128)S(1)}, f32[4,4096]{1,0:T(4,128)}, u32[]{:S(2)}) copy-start(f32[4,4096]{1,0:T(4,128)} %xd_in.1) | copy-start | bytes 196612
  0.9 0.7 copy-start.3
  1.6 2.8 %copy-start = (f32[4,4,128,128]{3,2,1,0:T(8,128)S(1)}, f32[4,4,128,128]{3,2,1,0:T(8,128)}, u32[]{:S(2)}) copy-start(f32[4,4,128,128]{3,2,1,0:T(8,128)} %state.1) | copy-start | bytes 3145732
  1.7 2.8 %copy-start.4 = (f32[4,4]{1,0:T(4,128)S(1)}, f32[4,4]{1,0:T(4,128)}, u32[]{:S(2)}) copy-start(f32[4,4]{1,0:T(4,128)} %kin.3) | copy-start | bytes 196
  1.7 2.8 %copy-start.5 = (f32[4,4]{1,0:T(4,128)S(1)}, f32[4,4]{1,0:T(4,128)}, u32[]{:S(2)}) copy-start(f32[4,4]{1,0:T(4,128)} %cross.3) | copy-start | bytes 196

commit v4 on v3

--- a/solution.py
+++ b/solution.py
@@ -36,7 +36,7 @@
 
 
 def tables_kernel(
-    nx, ny, xd_in, yd_in, gx, lx, hx, gy, ry, hy, wx, wx_cols, wy,
+    nx, ny, xd_in, yd_in, gx, lx, rx, hx, gy, ry, hy, wx, wx_cols, wy,
     rows_x, rows_y, ex, ey, p0, p1, q0, q1, xd, yd, arrived,
 ):
     k = lax.axis_index("row")
@@ -179,12 +179,16 @@
     wx[...] = jnp.where(
         rr % 16 == cc % 16, jnp.where(rr < 16, spread[0:1], spread[2:3]), 0.0
     )
-    width = nx * 8
-    spread = expand(width, 8, lambda r: r)
-    rr, cc = iota((16, width), 0), iota((16, width), 1)
-    wx_cols[...] = jnp.where(
-        rr % 8 == cc % 8, jnp.where(rr < 8, spread[0:1], spread[2:3]), 0.0
-    )
+    own_lanes = iota((nx, N), 1) // 4 == iota((nx, N), 0)
+    by_species = jnp.where(iota((N, N), 0) % 4 == iota((N, N), 1), 1.0, 0.0)
+    for p in range(2):
+        wx_cols[p] = lax.dot_general(
+            jnp.where(own_lanes, weight[2 * p : 2 * p + 1], 0.0),
+            by_species,
+            (((1,), (0,)), ((), ())),
+            precision=lax.Precision.HIGHEST,
+            preferred_element_type=f32,
+        )
     width = ny * 16
     spread = expand(width, 16, lambda r: r // 4)
     rr, cc = iota((32, width), 0), iota((32, width), 1)
@@ -215,43 +219,40 @@
     low = i0 >= j0
     r8 = iota((8, N), 0)
     c8 = iota((8, N), 1)
-    for s in range(4):
-        at = slice(32 + s, 33 + s)
-        pr, qr = phi_t[at], psi_t[at]
-        pc, qc, ec = phi[:, at], psi[:, at], eps[:, at]
-        pb, pa, qb, qa = phi_before[:, at], phi_after[:, at], psi_before[:, at], psi_after[:, at]
-        eq, ep = ec * qc, ec * pc
-        gx[s] = jnp.where(low, eq * pr, ep * qr)
-        lx[s] = jnp.where(j0 == 0, eq * pb, jnp.where(j0 == 1, ep * qa, 0.0))
+    def from_either_end(pr, qr, ends):
+        pb, pa, qb, qa = ends
         inv_p, inv_q = 1.0 / pr[:, N - 1 : N], 1.0 / qr[:, 0:1]
         beside = jnp.where(
             c8 == 0,
             pb * inv_p,
             jnp.where(c8 == 1, pa * inv_p, jnp.where(c8 == 2, qb * inv_q, qa * inv_q)),
         )
-        hx[s] = jnp.where(
+        return jnp.where(
             r8 == 0,
             pr * inv_p,
             jnp.where(r8 == 1, qr * inv_q, jnp.where(r8 == 2, beside, 0.0)),
         )
 
+    for s in range(4):
+        at = slice(32 + s, 33 + s)
+        pr, qr, er = phi_t[at], psi_t[at], eps_t[at]
+        pc, qc, ec = phi[:, at], psi[:, at], eps[:, at]
+        ends = phi_before[:, at], phi_after[:, at], psi_before[:, at], psi_after[:, at]
+        pb, pa, qb, qa = ends
+        eq, ep = ec * qc, ec * pc
+        gx[s] = jnp.where(low, eq * pr, ep * qr)
+        lx[s] = jnp.where(j0 == 0, eq * pb, jnp.where(j0 == 1, ep * qa, 0.0))
+        rx[s] = jnp.where(r8 == 0, pb * qr * er, jnp.where(r8 == 1, qa * pr * er, 0.0))
+        hx[s] = from_either_end(pr, qr, ends)
+
         at = slice(36 + s, 37 + s)
         pr, qr, er = phi_t[at], psi_t[at], eps_t[at]
         pc, qc = phi[:, at], psi[:, at]
-        pb, pa, qb, qa = phi_before[:, at], phi_after[:, at], psi_before[:, at], psi_after[:, at]
+        ends = phi_before[:, at], phi_after[:, at], psi_before[:, at], psi_after[:, at]
+        pb, pa, qb, qa = ends
         gy[s] = jnp.where(low, qc * (pr * er), pc * (qr * er))
         ry[s] = jnp.where(r8 == 0, pb * qr * er, jnp.where(r8 == 1, qa * pr * er, 0.0))
-        inv_p, inv_q = 1.0 / pr[:, N - 1 : N], 1.0 / qr[:, 0:1]
-        hy[s, :, 0:N] = jnp.where(
-            r8 == 0, pr * inv_p, jnp.where(r8 == 1, qr * inv_q, 0.0)
-        )
-        before = jnp.where(
-            r8 == 0, pb * inv_p, jnp.where(r8 == 1, qb * inv_q, jnp.where(r8 == 2, 1.0, 0.0))
-        )
-        after = jnp.where(
-            r8 == 0, pa * inv_p, jnp.where(r8 == 1, qa * inv_q, jnp.where(r8 == 3, 1.0, 0.0))
-        )
-        hy[s, :, N:] = jnp.where(c8 == 0, before, jnp.where(c8 == 1, after, 0.0))
+        hy[s] = from_either_end(pr, qr, ends)
 
 
 def by_plane(ref, p, s, values):
@@ -274,31 +275,29 @@
             tiles.append(t)
             laps.append(xm + xp + ym + yp - 4.0 * t)
         for j in range(4):
-            react = kin[0, j] * tiles[0]
-            mix = cross[0, j] * laps[0]
+            react = (0.5 * kin[0, j]) * tiles[0]
+            mix = (0.25 * cross[0, j]) * laps[0]
             for i in range(1, 4):
-                react = react + kin[i, j] * tiles[i]
-                mix = mix + cross[i, j] * laps[i]
-            f_out[j, :, z * N : (z + 1) * N] = (
-                tiles[j] + 0.5 * rate[j, z] * react + 0.25 * mix
-            )
-
-    side = []
+                react = react + (0.5 * kin[i, j]) * tiles[i]
+                mix = mix + (0.25 * cross[i, j]) * laps[i]
+            f_out[j, :, z * N : (z + 1) * N] = tiles[j] + rate[j, z] * react + mix
+
+    side = jnp.zeros((N, N), f32)
     for s in range(4):
-        acc = jnp.zeros((N, N), f32)
         for z in range(4):
-            tile = state[s, z]
-            acc = jnp.where(j0 == 8 * z, tile[:, 0:1], acc)
-            acc = jnp.where(j0 == 8 * z + 1, tile[:, N - 1 : N], acc)
-        side.append(acc)
-    has = jnp.where(j0 % 8 == 0, (l > 0).astype(f32), (l < ny - 1).astype(f32))
+            lane = 8 * s + 2 * z
+            side = jnp.where(j0 == lane, state[s, z, :, 0:1], side)
+            side = jnp.where(j0 == lane + 1, state[s, z, :, N - 1 : N], side)
+    side = side.T
+    r8, c8 = iota((8, N), 0), iota((8, N), 1)
+    has = 0.25 * jnp.where(r8 % 2 == 0, (l > 0).astype(f32), (l < ny - 1).astype(f32))
     has_x = 0.25 * (k > 0).astype(f32), 0.25 * (k < nx - 1).astype(f32)
-    pay[...] = jnp.zeros_like(pay)
+    tails = [jnp.zeros((8, N), f32)] * 2
     for j in range(4):
-        mix = cross[0, j] * side[0]
+        mix = cross[0, j] * side[0:8]
         for i in range(1, 4):
-            mix = mix + cross[i, j] * side[i]
-        mix = 0.25 * has * mix
+            mix = mix + cross[i, j] * side[8 * i : 8 * i + 8]
+        mix = has * mix
         cols[j] = mix
         beside = []
         for p, row in enumerate((0, N - 1)):
@@ -311,30 +310,37 @@
             beside.append(jnp.concatenate(pieces, axis=1))
             by_plane(cells, p, j, beside[p])
         sums = dot3(hx[j], f_out[j])
-        ends = dot3(hx[j], mix)
         for p in range(2):
             c = hx[j, 2:3, 2 * p : 2 * p + 1], hx[j, 2:3, 2 * p + 1 : 2 * p + 2]
             by_plane(pay, p, j, sums[p : p + 1] + c[0] * beside[0] + c[1] * beside[1])
-            pay[p, 16 + j : 17 + j, :] = ends[p : p + 1]
+            total = jnp.sum(mix * hx[j, p : p + 1, :], axis=1, keepdims=True)
+            tails[p] = jnp.where(c8 == j, total, tails[p])
+    for p in range(2):
+        pay[p, 16:24, :] = tails[p]
     for j in range(nx):
         send[j] = pay[(j < k).astype(jnp.int32)]
 
 
 def rows_kernel(
-    nx, ny, f_in, cells, cols, recv, wx, wx_cols, gx, lx, hy, g_out, send, beside, pay
+    nx, ny, f_in, cells, cols, recv, wx, wx_cols, gx, lx, rx, hy, g_out, send, beside, pay
 ):
     l = lax.axis_index("col")
     incoming = dot3(wx[...], recv[:, 0:16, :].reshape(nx * 16, N))
-    in_cols = dot3(wx_cols[...], recv[:, 16:24, :].reshape(nx * 8, N))
     from_before = incoming[0:16] + cells[0]
     from_after = incoming[16:32] + cells[1]
+    in_cols = []
+    for p in range(2):
+        total = recv[0, 16:24, :] * wx_cols[p, 0:1, :]
+        for j in range(1, nx):
+            total = total + recv[j, 16:24, :] * wx_cols[p, j : j + 1, :]
+        in_cols.append(total)
     for s in range(4):
         g = dot3(gx[s], f_in[s])
         lam, mu = lx[s, :, 0:1], lx[s, :, 1:2]
         col = (
-            dot3(gx[s], cols[s])
-            + lam * in_cols[s : s + 1]
-            + mu * in_cols[8 + s : 9 + s]
+            dot3(cols[s], gx[s], nt=True)
+            + in_cols[0][:, s : s + 1] * rx[s, 0:1]
+            + in_cols[1][:, s : s + 1] * rx[s, 1:2]
         )
         parts = []
         for z in range(4):
@@ -343,12 +349,17 @@
                 g[:, z * N : (z + 1) * N] + lam * from_before[q] + mu * from_after[q]
             )
             g_out[s, z] = part
-            edge = col if z == 0 else pltpu.roll(col, N - 8 * z, 1)
-            parts.append(jnp.concatenate([part, edge], axis=1))
+            parts.append(part)
         ends = dot3(hy[s], jnp.concatenate(parts, axis=0), nt=True)
         for p in range(2):
-            by_plane(pay, p, s, ends[p : p + 1])
-            by_plane(beside, p, s, ends[2 + p : 3 + p])
+            c = hy[s, 2:3, 2 * p : 2 * p + 1], hy[s, 2:3, 2 * p + 1 : 2 * p + 2]
+            for z in range(4):
+                q = slice(4 * s + z, 4 * s + z + 1)
+                before, after = col[2 * z : 2 * z + 1], col[2 * z + 1 : 2 * z + 2]
+                pay[p, q, :] = (
+                    ends[p : p + 1, z * N : (z + 1) * N] + c[0] * before + c[1] * after
+                )
+                beside[p, q, :] = after if p else before
     for m in range(ny):
         send[m] = pay[(m < l).astype(jnp.int32)]
 
@@ -410,17 +421,17 @@
 def on_device(adjoint, rate_scale, kinetics, cross_matrix, x_diffusion, y_diffusion):
     nx, ny = lax.axis_size("row"), lax.axis_size("col")
     part = functools.partial
-    gx, lx, hx, gy, ry, hy, wx, wx_cols, wy = call(
+    gx, lx, rx, hx, gy, ry, hy, wx, wx_cols, wy = call(
         part(tables_kernel, nx, ny),
         [
-            (4, N, N), (4, N, N), (4, 8, N), (4, N, N), (4, 8, N), (4, 8, 2 * N),
-            (32, nx * 16), (16, nx * 8), (32, ny * 16),
+            (4, N, N), (4, N, N), (4, 8, N), (4, 8, N), (4, N, N), (4, 8, N), (4, 8, N),
+            (32, nx * 16), (2, nx, N), (32, ny * 16),
         ],
         [(N, N)] * 8 + [x_diffusion.shape, y_diffusion.shape, pltpu.SemaphoreType.DMA((2,))],
-        place=pl.ANY,
+        place=pltpu.HBM,
     )(x_diffusion, y_diffusion)
     tile = (4, 4, N, N)
-    step_out = [(4, N, 4 * N), (nx, 24, N), (2, 16, N), (4, N, N)]
+    step_out = [(4, N, 4 * N), (nx, 24, N), (2, 16, N), (4, 8, N)]
     f, send, cells, cols = call(part(explicit, nx, ny), step_out, [(2, 24, N)], 2)(
         adjoint, rate_scale, hx, kinetics, cross_matrix
     )
@@ -428,7 +439,7 @@
         recv = lax.all_to_all(send, "row", 0, 0, tiled=True)
         g, send, beside = call(
             part(rows_kernel, nx, ny), [tile, (ny, 16, N), (2, 16, N)], [(2, 16, N)]
-        )(f, cells, cols, recv, wx, wx_cols, gx, lx, hy)
+        )(f, cells, cols, recv, wx, wx_cols, gx, lx, rx, hy)
         recv = lax.all_to_all(send, "col", 0, 0, tiled=True)
         if step + 1 < STEPS:
             f, send, cells, cols = call(

time: 76.4 us -> 74.3 us (0.973)
  Pallas kernels: 15.8 us -> 13.8 us
    pallas_call x6, Pallas kernels: 15.8 us -> 13.8 us  [run(): pl.pallas_call(body, out_shape=shapes, in_specs=[pl.BlockSpec(memory_spac...]
where the time goes in v4:
time: 74.3 us; the launch traced here: 74 us
  blocking collectives  58.5 us (79%)
  Pallas kernels  13.8 us (19%)
  local copies, waits for them, and re-layouts  1.66 us (2%)
    all_to_all x2, blocking collectives, on_device(): recv = lax.all_to_all(send, 'row', 0, 0, tiled=True)  33.7 us
    all_to_all x2, blocking collectives, on_device(): recv = lax.all_to_all(send, 'col', 0, 0, tiled=True)  24.7 us
    pallas_call x6, Pallas kernels, run(): pl.pallas_call(body, out_shape=shapes, in_specs=[pl.BlockSpec(memory_spac...  13.8 us
    unnamed x12, local copies, waits for them, and re-layouts  1.66 us

profile of v4, /device:TPU:1, one launch (start us, length us, event | category | flops | bytes accessed | tf_op | source)
XLA Modules:
  0.0 74.0 jit_solution(8168836818138588503)
XLA Ops:
  0.0 0.0 copy-start.1
  0.0 0.0 copy-start.2
  0.0 0.9 %copy-done.2 = f32[4,4096]{1,0:T(4,128)S(1)} copy-done((f32[4,4096]{1,0:T(4,128)S(1)}, f32[4,4096]{1,0:T(4,128)}, u32[]{:S(2)}) %copy-start.2) | copy-done | bytes 65560
  0.9 0.0 copy-start.3
  0.9 0.7 copy-done.3
  1.6 0.0 copy-start
  1.7 0.0 copy-start.4
  1.7 0.0 copy-start.5
  1.7 2.7 %shard_map.64 = (f32[4,128,128]{2,1,0:T(8,128)S(1)}, f32[4,128,128]{2,1,0:T(8,128)S(1)}, f32[4,8,128]{2,1,0:T(8,128)S(1)}, f32[4,8,128]{2,1,0:T(8,128)S(1)}, f32...) custom-call(f32[4,4096]{1,0:T(4,128)S(1)} %copy-done.2, ...), custom_call_target="tpu_custom_call" | custom-call | flops 3000000000 | bytes 3000000 | tf_op jit(solution)/shard_map/pallas_call | solution.py:402
  4.4 0.0 copy-done.1
  4.4 0.0 copy-done
  4.4 0.0 copy-done.4
  4.4 0.0 copy-done.5
  4.4 2.6 %shard_map.65 = (f32[4,128,512]{2,1,0:T(8,128)S(1)}, f32[32,24,128]{2,1,0:T(8,128)S(1)}, f32[2,16,128]{2,1,0:T(8,128)S(1)}, f32[4,8,128]{2,1,0:T(8,128)S(1)}) custom-call(f32[4,4,128,128]{3,2,1,0:T(8,128)S(1)} %copy-done, f32[4,4,128,128]{3,2,1,0:T(8,128)S(1)} %copy-done.1, f32[4,8,128]{2,1,0:T(8,128)S(1)} %get-tuple-element.29.hx, f32[4,4]{1,0:T(4,128)S(1)} %copy-done.4, ...), custom_call_target="tpu_custom_call" | custom-call | flops 3000000000 | bytes 3000000 | tf_op jit(solution)/shard_map/pallas_call | solution.py:402
  7.0 18.6 %all_to_all.20.recv = f32[32,24,128]{2,1,0:T(8,128)S(1)} all-to-all(f32[32,24,128]{2,1,0:T(8,128)S(1)} %get-tuple-element.33), channel_id=1, replica_groups=mesh['row'=32,'col'=8] {'row'}, dimensions={0} | all-to-all | bytes 786432 | tf_op jit(solution)/shard_map/all_to_all | solution.py:439
  25.6 1.5 %shard_map.66 = (f32[4,4,128,128]{3,2,1,0:T(8,128)S(1)}, f32[8,16,128]{2,1,0:T(8,128)S(1)}, f32[2,16,128]{2,1,0:T(8,128)S(1)}) custom-call(f32[4,128,512]{2,1,0:T(8,128)S(1)} %get-tuple-element.30.f_in, f32[2,16,128]{2,1,0:T(8,128)S(1)} %get-tuple-element.31.cells, f32[4,8,128]{2,1,0:T(8,128)S(1)} %get-tuple-element.32.cols, ...), custom_call_target="tpu_custom_call" | custom-call | flops 3000000000 | bytes 3000000 | tf_op jit(solution)/shard_map/pallas_call | solution.py:402
  27.1 15.2 %all_to_all.21.recv = f32[8,16,128]{2,1,0:T(8,128)S(1)} all-to-all(f32[8,16,128]{2,1,0:T(8,128)S(1)} %get-tuple-element.41), channel_id=1, replica_groups=mesh['row'=32,'col'=8] {'col'}, dimensions={0} | all-to-all | bytes 131072 | tf_op jit(solution)/shard_map/all_to_all | solution.py:443
  42.3 3.5 %shard_map.67 = (f32[4,128,512]{2,1,0:T(8,128)S(1)}, f32[32,24,128]{2,1,0:T(8,128)S(1)}, f32[2,16,128]{2,1,0:T(8,128)S(1)}, f32[4,8,128]{2,1,0:T(8,128)S(1)}) custom-call(f32[4,4,128,128]{3,2,1,0:T(8,128)S(1)} %get-tuple-element.40.g_in, f32[8,16,128]{2,1,0:T(8,128)S(1)} %all_to_all.21.recv, f32[2,16,128]{2,1,0:T(8,128)S(1)} %get-tuple-element.42.beside, ...), custom_call_target="tpu_custom_call" | custom-call | flops 3000000000 | bytes 3000000 | tf_op jit(solution)/shard_map/pallas_call | solution.py:402
  45.8 15.2 %all_to_all.22.recv = f32[32,24,128]{2,1,0:T(8,128)S(1)} all-to-all(f32[32,24,128]{2,1,0:T(8,128)S(1)} %get-tuple-element.49), channel_id=1, replica_groups=mesh['row'=32,'col'=8] {'row'}, dimensions={0} | all-to-all | bytes 786432 | tf_op jit(solution)/shard_map/all_to_all | solution.py:439
  61.0 1.5 %shard_map.68 = (f32[4,4,128,128]{3,2,1,0:T(8,128)S(1)}, f32[8,16,128]{2,1,0:T(8,128)S(1)}, f32[2,16,128]{2,1,0:T(8,128)S(1)}) custom-call(f32[4,128,512]{2,1,0:T(8,128)S(1)} %get-tuple-element.46.f_in, f32[2,16,128]{2,1,0:T(8,128)S(1)} %get-tuple-element.47.cells, f32[4,8,128]{2,1,0:T(8,128)S(1)} %get-tuple-element.48.cols, ...), custom_call_target="tpu_custom_call" | custom-call | flops 3000000000 | bytes 3000000 | tf_op jit(solution)/shard_map/pallas_call | solution.py:402
  62.5 9.5 %all_to_all.23.recv = f32[8,16,128]{2,1,0:T(8,128)S(1)} all-to-all(f32[8,16,128]{2,1,0:T(8,128)S(1)} %get-tuple-element.51), channel_id=1, replica_groups=mesh['row'=32,'col'=8] {'col'}, dimensions={0} | all-to-all | bytes 131072 | tf_op jit(solution)/shard_map/all_to_all | solution.py:443
  72.0 2.0 %shard_map.69 = f32[4,4,128,128]{3,2,1,0:T(8,128)} custom-call(f32[4,4,128,128]{3,2,1,0:T(8,128)S(1)} %get-tuple-element.50.g_in, f32[8,16,128]{2,1,0:T(8,128)S(1)} %all_to_all.23.recv, f32[2,16,128]{2,1,0:T(8,128)S(1)} %get-tuple-element.52.beside, f32[32,128]{1,0:T(8,128)S(1)} %get-tuple-element.43.wy, f32[4,128,128]{2,1,0:T(8,128)S(1)} %get-tuple-element.44.gy, ...), custom_call_target="tpu_custom_call" | custom-call | flops 3000000000 | bytes 3000000 | tf_op jit(solution)/shard_map/pallas_call | solution.py:402
Async XLA Ops:
  0.0 4.4 %copy-start.1 = (f32[4,4,128,128]{3,2,1,0:T(8,128)S(1)}, f32[4,4,128,128]{3,2,1,0:T(8,128)}, u32[]{:S(2)}) copy-start(f32[4,4,128,128]{3,2,1,0:T(8,128)} %rate.3) | copy-start | bytes 3145732
  0.0 0.9 %copy-start.2 = (f32[4,4096]{1,0:T(4,128)S(1)}, f32[4,4096]{1,0:T(4,128)}, u32[]{:S(2)}) copy-start(f32[4,4096]{1,0:T(4,128)} %xd_in.1) | copy-start | bytes 196612
  0.9 0.7 copy-start.3
  1.6 2.7 %copy-start = (f32[4,4,128,128]{3,2,1,0:T(8,128)S(1)}, f32[4,4,128,128]{3,2,1,0:T(8,128)}, u32[]{:S(2)}) copy-start(f32[4,4,128,128]{3,2,1,0:T(8,128)} %state.1) | copy-start | bytes 3145732
  1.7 2.7 %copy-start.4 = (f32[4,4]{1,0:T(4,128)S(1)}, f32[4,4]{1,0:T(4,128)}, u32[]{:S(2)}) copy-start(f32[4,4]{1,0:T(4,128)} %kin.3) | copy-start | bytes 196
  1.7 2.7 %copy-start.5 = (f32[4,4]{1,0:T(4,128)S(1)}, f32[4,4]{1,0:T(4,128)}, u32[]{:S(2)}) copy-start(f32[4,4]{1,0:T(4,128)} %cross.3) | copy-start | bytes 196

commit v5 on v4

--- a/solution.py
+++ b/solution.py
@@ -10,6 +10,7 @@
 M = 1000.0
 STEPS = 2
 N = 128
+STRIP = 32
 f32 = jnp.float32
 bf16 = jnp.bfloat16
 VMEM = 20 * 1024 * 1024
@@ -20,51 +21,82 @@
 
 
 def split(a):
-    hi = a.astype(bf16)
-    return hi, (a - hi.astype(f32)).astype(bf16)
-
-
-def dot3(a, b, nt=False):
+    hi = a.astype(bf16).astype(f32)
+    return hi, a - hi
+
+
+def bdot(a, b, nt=False):
     dims = (((1,), (1 if nt else 0,)), ((), ()))
+    return lax.dot_general(
+        a.astype(bf16), b.astype(bf16), dims, preferred_element_type=f32
+    )
+
+
+def dot_rows(a, b, nt=False):
     ah, al = split(a)
     bh, bl = split(b)
-
-    def dot(p, q):
-        return lax.dot_general(p, q, dims, preferred_element_type=f32)
-
-    return dot(ah, bh) + (dot(ah, bl) + dot(al, bh))
+    n = a.shape[0]
+    left = jnp.concatenate(
+        [jnp.concatenate([ah, ah], axis=1), jnp.concatenate([al, al], axis=1)], axis=0
+    )
+    out = bdot(left, jnp.concatenate([bh, bl], axis=1 if nt else 0), nt)
+    return out[0:n] + out[n:]
+
+
+def dot_cols(a, b):
+    ah, al = split(a)
+    bh, bl = split(b)
+    n = b.shape[1]
+    right = jnp.concatenate([bh, bl], axis=1)
+    out = bdot(
+        jnp.concatenate([ah, al], axis=1), jnp.concatenate([right, right], axis=0)
+    )
+    return out[:, 0:n] + out[:, n:]
+
+
+def dot_mixed(a, b):
+    ah, al = split(a)
+    bh, bl = split(b)
+    m, n = a.shape[0], b.shape[1]
+    out = bdot(jnp.concatenate([ah, al], axis=0), jnp.concatenate([bh, bl], axis=1))
+    return (out[0:m, 0:n] + out[m:, n:]) + (out[0:m, n:] + out[m:, 0:n])
+
+
+def pick(a, hit):
+    hi, rest = split(a)
+    mid, low = split(rest)
+    n = a.shape[0]
+    out = bdot(jnp.concatenate([hi, mid, low], axis=0), jnp.where(hit, 1.0, 0.0))
+    return (out[0:n] + out[n : 2 * n]) + out[2 * n :]
 
 
 def tables_kernel(
-    nx, ny, xd_in, yd_in, gx, lx, rx, hx, gy, ry, hy, wx, wx_cols, wy,
-    rows_x, rows_y, ex, ey, p0, p1, q0, q1, xd, yd, arrived,
+    nx, ny, eps_all, gx, lx, rx, hx, gy, ry, hy, wx, wx_cols, wy,
+    rows_x, rows_y, ex, ey, p0, p1, q0, q1,
 ):
     k = lax.axis_index("row")
     l = lax.axis_index("col")
-    scale = 1.0 / M
-    x_copy = pltpu.make_async_copy(xd_in, xd, arrived.at[0])
-    y_copy = pltpu.make_async_copy(yd_in, yd, arrived.at[1])
-    x_copy.start()
-    y_copy.start()
-    rows_x[...] = jnp.full((N, N), scale, f32)
-    rows_y[...] = jnp.full((N, N), scale, f32)
-    x_copy.wait()
-    y_copy.wait()
+    rows_x[...] = jnp.full((N, N), 1.0 / M, f32)
+    rows_y[...] = jnp.full((N, N), 1.0 / M, f32)
     for j in range(nx):
-        rows_x[4 * j : 4 * j + 4, :] = scale / xd[:, j * N : (j + 1) * N]
+        rows_x[4 * j : 4 * j + 4, :] = eps_all[:, j * N : (j + 1) * N]
     for j in range(ny):
-        rows_y[4 * j : 4 * j + 4, :] = scale / yd[:, j * N : (j + 1) * N]
-
-    def block(ref, index):
-        return scale / ref[:, pl.ds(pl.multiple_of(index * N, N), N)]
-
-    rows_y[32:36, :] = block(xd, k)
-    rows_y[36:40, :] = block(yd, l)
+        rows_y[4 * j : 4 * j + 4, :] = eps_all[:, (nx + j) * N : (nx + j + 1) * N]
+
+    def block(index):
+        return eps_all[:, pl.ds(pl.multiple_of(index * N, N), N)]
+
+    rows_y[32:36, :] = block(k)
+    rows_y[36:40, :] = block(nx + l)
     ex[...] = rows_x[...].T
     ey[...] = rows_y[...].T
 
     first2 = (iota((2, N), 0) == 0).astype(f32)
     one, zero = jnp.ones((1, N), f32), jnp.zeros((1, N), f32)
+
+    def advance(e, v, d):
+        grown = e * v
+        return (v + d) + grown, d + grown
 
     def body(i, carry):
         vx, dx, va, da, vb, db, ux, cx, ua, ca, ub, cb = carry
@@ -77,23 +109,17 @@
             p0[pl.ds(t, 1), :] = va
             p1[pl.ds(t, 1), :] = vb
             e, ee = ex_f[r : r + 1], ey_f[r : r + 1]
-            dx = dx + e * vx
-            vx = vx + dx
-            da = da + ee * va
-            va = va + da
-            db = db + ee * vb
-            vb = vb + db
+            vx, dx = advance(e, vx, dx)
+            va, da = advance(ee, va, da)
+            vb, db = advance(ee, vb, db)
             r2 = 7 - r
             t = back + r2
             q0[pl.ds(t, 1), :] = ua
             q1[pl.ds(t, 1), :] = ub
             e, ee = ex_b[r2 : r2 + 1], ey_b[r2 : r2 + 1]
-            cx = cx + e * ux
-            ux = ux + cx
-            ca = ca + ee * ua
-            ua = ua + ca
-            cb = cb + ee * ub
-            ub = ub + cb
+            ux, cx = advance(e, ux, cx)
+            ua, ca = advance(ee, ua, ca)
+            ub, cb = advance(ee, ub, cb)
         return vx, dx, va, da, vb, db, ux, cx, ua, ca, ub, cb
 
     init = (first2, 1.0 - first2, one, zero, zero, one)
@@ -137,9 +163,10 @@
         sc = jnp.where(skip, 0.0, shifted(c, by))
         sd = jnp.where(skip, 1.0, shifted(d, by))
         a, b, c, d = a * sa + b * sc, a * sb + b * sd, c * sa + d * sc, c * sb + d * sd
-        norm = 1.0 / (a + b)
-        a, b, c, d = a * norm, b * norm, c * norm, d * norm
         by *= 2
+        if by == 16:
+            norm = 1.0 / (a + b)
+            a, b, c, d = a * norm, b * norm, c * norm, d * norm
     skip = outside(1)
     slope = jnp.where(skip, 1.0, shifted((c + d) / (a + b), 1))
 
@@ -165,13 +192,7 @@
         src = iota((N, width), 0)
         col = iota((N, width), 1)
         hit = (src // 4 == col // per_block) & (src % 4 == species_of(col % per_block))
-        return lax.dot_general(
-            weight,
-            jnp.where(hit, 1.0, 0.0),
-            (((1,), (0,)), ((), ())),
-            precision=lax.Precision.HIGHEST,
-            preferred_element_type=f32,
-        )
+        return pick(weight, hit)
 
     width = nx * 16
     spread = expand(width, 16, lambda r: r // 4)
@@ -180,14 +201,10 @@
         rr % 16 == cc % 16, jnp.where(rr < 16, spread[0:1], spread[2:3]), 0.0
     )
     own_lanes = iota((nx, N), 1) // 4 == iota((nx, N), 0)
-    by_species = jnp.where(iota((N, N), 0) % 4 == iota((N, N), 1), 1.0, 0.0)
+    by_species = iota((N, N), 0) % 4 == iota((N, N), 1)
     for p in range(2):
-        wx_cols[p] = lax.dot_general(
-            jnp.where(own_lanes, weight[2 * p : 2 * p + 1], 0.0),
-            by_species,
-            (((1,), (0,)), ((), ())),
-            precision=lax.Precision.HIGHEST,
-            preferred_element_type=f32,
+        wx_cols[p] = pick(
+            jnp.where(own_lanes, weight[2 * p : 2 * p + 1], 0.0), by_species
         )
     width = ny * 16
     spread = expand(width, 16, lambda r: r // 4)
@@ -263,34 +280,44 @@
 
 def explicit(nx, ny, state, rate, hx, kin, cross, f_out, send, cells, cols, pay):
     k, l = lax.axis_index("row"), lax.axis_index("col")
-    i0, j0 = iota((N, N), 0), iota((N, N), 1)
+    j0 = iota((N, N), 1)
+    ri, rj = iota((STRIP, N), 0), iota((STRIP, N), 1)
     for z in range(4):
-        tiles, laps = [], []
-        for s in range(4):
-            t = state[s, z]
-            xm = jnp.where(i0 == 0, 0.0, pltpu.roll(t, 1, 0))
-            xp = jnp.where(i0 == N - 1, 0.0, pltpu.roll(t, N - 1, 0))
-            ym = jnp.where(j0 == 0, 0.0, pltpu.roll(t, 1, 1))
-            yp = jnp.where(j0 == N - 1, 0.0, pltpu.roll(t, N - 1, 1))
-            tiles.append(t)
-            laps.append(xm + xp + ym + yp - 4.0 * t)
-        for j in range(4):
-            react = (0.5 * kin[0, j]) * tiles[0]
-            mix = (0.25 * cross[0, j]) * laps[0]
-            for i in range(1, 4):
-                react = react + (0.5 * kin[i, j]) * tiles[i]
-                mix = mix + (0.25 * cross[i, j]) * laps[i]
-            f_out[j, :, z * N : (z + 1) * N] = tiles[j] + rate[j, z] * react + mix
+        for at in range(0, N, STRIP):
+            end = at + STRIP
+            tiles, laps = [], []
+            for s in range(4):
+                t = state[s, z, at:end, :]
+                if at == 0:
+                    xm = jnp.where(ri == 0, 0.0, pltpu.roll(t, 1, 0))
+                else:
+                    xm = state[s, z, at - 1 : end - 1, :]
+                if end == N:
+                    xp = jnp.where(ri == STRIP - 1, 0.0, pltpu.roll(t, STRIP - 1, 0))
+                else:
+                    xp = state[s, z, at + 1 : end + 1, :]
+                ym = jnp.where(rj == 0, 0.0, pltpu.roll(t, 1, 1))
+                yp = jnp.where(rj == N - 1, 0.0, pltpu.roll(t, N - 1, 1))
+                tiles.append(t)
+                laps.append(xm + xp + ym + yp - 4.0 * t)
+            for j in range(4):
+                react = (0.5 * kin[0, j]) * tiles[0]
+                mix = (0.25 * cross[0, j]) * laps[0]
+                for i in range(1, 4):
+                    react = react + (0.5 * kin[i, j]) * tiles[i]
+                    mix = mix + (0.25 * cross[i, j]) * laps[i]
+                f_out[j, at:end, z * N : (z + 1) * N] = (
+                    tiles[j] + rate[j, z, at:end, :] * react + mix
+                )
 
     side = jnp.zeros((N, N), f32)
     for s in range(4):
         for z in range(4):
-            lane = 8 * s + 2 * z
-            side = jnp.where(j0 == lane, state[s, z, :, 0:1], side)
-            side = jnp.where(j0 == lane + 1, state[s, z, :, N - 1 : N], side)
+            q = 4 * s + z
+            side = jnp.where(j0 // 2 == q, pltpu.roll(state[s, z], 2 * q + 1, 1), side)
     side = side.T
     r8, c8 = iota((8, N), 0), iota((8, N), 1)
-    has = 0.25 * jnp.where(r8 % 2 == 0, (l > 0).astype(f32), (l < ny - 1).astype(f32))
+    has = 0.25 * jnp.where(r8 % 2 == 0, (l < ny - 1).astype(f32), (l > 0).astype(f32))
     has_x = 0.25 * (k > 0).astype(f32), 0.25 * (k < nx - 1).astype(f32)
     tails = [jnp.zeros((8, N), f32)] * 2
     for j in range(4):
@@ -309,7 +336,7 @@
                 pieces.append(has_x[p] * piece)
             beside.append(jnp.concatenate(pieces, axis=1))
             by_plane(cells, p, j, beside[p])
-        sums = dot3(hx[j], f_out[j])
+        sums = dot_rows(hx[j], f_out[j])
         for p in range(2):
             c = hx[j, 2:3, 2 * p : 2 * p + 1], hx[j, 2:3, 2 * p + 1 : 2 * p + 2]
             by_plane(pay, p, j, sums[p : p + 1] + c[0] * beside[0] + c[1] * beside[1])
@@ -325,7 +352,7 @@
     nx, ny, f_in, cells, cols, recv, wx, wx_cols, gx, lx, rx, hy, g_out, send, beside, pay
 ):
     l = lax.axis_index("col")
-    incoming = dot3(wx[...], recv[:, 0:16, :].reshape(nx * 16, N))
+    incoming = dot_mixed(wx[...], recv[:, 0:16, :].reshape(nx * 16, N))
     from_before = incoming[0:16] + cells[0]
     from_after = incoming[16:32] + cells[1]
     in_cols = []
@@ -335,10 +362,10 @@
             total = total + recv[j, 16:24, :] * wx_cols[p, j : j + 1, :]
         in_cols.append(total)
     for s in range(4):
-        g = dot3(gx[s], f_in[s])
+        g = dot_rows(gx[s], f_in[s])
         lam, mu = lx[s, :, 0:1], lx[s, :, 1:2]
         col = (
-            dot3(cols[s], gx[s], nt=True)
+            dot_rows(cols[s], gx[s], nt=True)
             + in_cols[0][:, s : s + 1] * rx[s, 0:1]
             + in_cols[1][:, s : s + 1] * rx[s, 1:2]
         )
@@ -350,12 +377,12 @@
             )
             g_out[s, z] = part
             parts.append(part)
-        ends = dot3(hy[s], jnp.concatenate(parts, axis=0), nt=True)
+        ends = dot_rows(hy[s], jnp.concatenate(parts, axis=0), nt=True)
         for p in range(2):
             c = hy[s, 2:3, 2 * p : 2 * p + 1], hy[s, 2:3, 2 * p + 1 : 2 * p + 2]
             for z in range(4):
                 q = slice(4 * s + z, 4 * s + z + 1)
-                before, after = col[2 * z : 2 * z + 1], col[2 * z + 1 : 2 * z + 2]
+                after, before = col[2 * z : 2 * z + 1], col[2 * z + 1 : 2 * z + 2]
                 pay[p, q, :] = (
                     ends[p : p + 1, z * N : (z + 1) * N] + c[0] * before + c[1] * after
                 )
@@ -364,8 +391,8 @@
         send[m] = pay[(m < l).astype(jnp.int32)]
 
 
-def finish_cols(ny, g_in, recv, beside, wy, gy, ry, out, turned):
-    incoming = dot3(wy[...], recv[...].reshape(ny * 16, N))
+def finish_cols(ny, g_in, recv, beside, wy, gy, ry, out, turned, done=None):
+    incoming = dot_mixed(wy[...], recv[...].reshape(ny * 16, N))
     turned[...] = jnp.concatenate(
         [
             incoming[0:16] + beside[0],
@@ -375,7 +402,7 @@
         axis=0,
     ).T
     for s in range(4):
-        res = dot3(g_in[s].reshape(4 * N, N), gy[s])
+        res = dot_cols(g_in[s].reshape(4 * N, N), gy[s])
         lam, mu = ry[s, 0:1], ry[s, 1:2]
         for z in range(4):
             q = 4 * s + z
@@ -384,6 +411,19 @@
                 + turned[:, q : q + 1] * lam
                 + turned[:, 16 + q : 17 + q] * mu
             )
+        if done is not None:
+            done(s)
+
+
+def last_kernel(ny, g_in, recv, beside, wy, gy, ry, out, state, turned, sent):
+    copies = [
+        pltpu.make_async_copy(state.at[s], out.at[s], sent.at[s]) for s in range(4)
+    ]
+    finish_cols(
+        ny, g_in, recv, beside, wy, gy, ry, state, turned, lambda s: copies[s].start()
+    )
+    for copy in copies:
+        copy.wait()
 
 
 def next_kernel(
@@ -394,7 +434,7 @@
     explicit(nx, ny, state, rate, hx, kin, cross, f_out, send, cells, cols, pay)
 
 
-def call(body, outs, scratch, smem=0, place=pltpu.VMEM):
+def call(body, outs, scratch, smem=0, place_out=pltpu.VMEM):
     shapes = [jax.ShapeDtypeStruct(shape, f32) for shape in outs]
 
     def run(*args):
@@ -402,9 +442,9 @@
         return pl.pallas_call(
             body,
             out_shape=shapes,
-            in_specs=[pl.BlockSpec(memory_space=place)] * count
+            in_specs=[pl.BlockSpec(memory_space=pltpu.VMEM)] * count
             + [pl.BlockSpec(memory_space=pltpu.SMEM)] * smem,
-            out_specs=[pl.BlockSpec(memory_space=pltpu.VMEM)] * len(shapes),
+            out_specs=[pl.BlockSpec(memory_space=place_out)] * len(shapes),
             scratch_shapes=[
                 pltpu.VMEM(shape, f32) if isinstance(shape, tuple) else shape
                 for shape in scratch
@@ -427,9 +467,8 @@
             (4, N, N), (4, N, N), (4, 8, N), (4, 8, N), (4, N, N), (4, 8, N), (4, 8, N),
             (32, nx * 16), (2, nx, N), (32, ny * 16),
         ],
-        [(N, N)] * 8 + [x_diffusion.shape, y_diffusion.shape, pltpu.SemaphoreType.DMA((2,))],
-        place=pltpu.HBM,
-    )(x_diffusion, y_diffusion)
+        [(N, N)] * 8,
+    )(1.0 / (M * jnp.concatenate([x_diffusion, y_diffusion], axis=1)))
     tile = (4, 4, N, N)
     step_out = [(4, N, 4 * N), (nx, 24, N), (2, 16, N), (4, 8, N)]
     f, send, cells, cols = call(part(explicit, nx, ny), step_out, [(2, 24, N)], 2)(
@@ -445,7 +484,12 @@
             f, send, cells, cols = call(
                 part(next_kernel, nx, ny), step_out, [tile, (N, N), (2, 24, N)], 2
             )(g, recv, beside, wy, gy, ry, rate_scale, hx, kinetics, cross_matrix)
-    (out,) = call(part(finish_cols, ny), [tile], [(N, N)])(g, recv, beside, wy, gy, ry)
+    (out,) = call(
+        part(last_kernel, ny),
+        [tile],
+        [tile, (N, N), pltpu.SemaphoreType.DMA((4,))],
+        place_out=pl.ANY,
+    )(g, recv, beside, wy, gy, ry)
     return out
 
 

time: 74.3 us -> 71.6 us (0.964)
  Pallas kernels: 13.8 us -> 11.8 us
  local copies, waits for them, and re-layouts: 1.66 us -> 0.03 us
  other arithmetic: 0 us -> 0.89 us
    pallas_call x6, Pallas kernels: 13.8 us -> 11.8 us  [run(): pl.pallas_call(body, out_shape=shapes, in_specs=[pl.BlockSpec(memory_spac...]
    unnamed x12 -> x8, local copies, waits for them, and re-layouts: 1.66 us -> 0.03 us
    div x0 -> x1, other arithmetic: none -> 0.89 us  [on_device(): 1.0 / (M * jnp.concatenate([x_diffusion, y_diffusion], axis=1))]
where the time goes in v5:
time: 71.6 us; the launch traced here: 71.3 us
  blocking collectives  58.5 us (82%)
  Pallas kernels  11.8 us (16%)
  other arithmetic  0.89 us (1%)
    all_to_all x2, blocking collectives, on_device(): recv = lax.all_to_all(send, 'row', 0, 0, tiled=True)  33.7 us
    all_to_all x2, blocking collectives, on_device(): recv = lax.all_to_all(send, 'col', 0, 0, tiled=True)  24.7 us
    pallas_call x6, Pallas kernels, run(): pl.pallas_call(body, out_shape=shapes, in_specs=[pl.BlockSpec(memory_spac...  11.8 us

profile of v5, /device:TPU:1, one launch (start us, length us, event | category | flops | bytes accessed | tf_op | source)
XLA Modules:
  0.0 71.3 jit_solution(13945653060525102534)
XLA Ops:
  0.0 0.9 %fusion.eps_all = f32[4,5120]{1,0:T(4,128)S(1)} fusion(f32[4,1024]{1,0:T(4,128)} %param.11, f32[4,4096]{1,0:T(4,128)} %param.10), kind=kLoop, calls=%fused_computation.1 | loop fusion | flops 61440 | bytes 163840 | tf_op jit(solution)/shard_map/div | solution.py:471
  0.9 0.0 copy-start
  0.9 0.0 copy-start.1
  0.9 0.0 copy-start.2
  0.9 0.0 copy-start.3
  0.9 2.3 %shard_map.64 = (f32[4,128,128]{2,1,0:T(8,128)S(1)}, f32[4,128,128]{2,1,0:T(8,128)S(1)}, f32[4,8,128]{2,1,0:T(8,128)S(1)}, f32[4,8,128]{2,1,0:T(8,128)S(1)}, f32...) custom-call(f32[4,5120]{1,0:T(4,128)S(1)} %fusion.eps_all), custom_call_target="tpu_custom_call" | custom-call | flops 3000000000 | bytes 3000000 | tf_op jit(solution)/shard_map/pallas_call | solution.py:442
  3.2 0.0 copy-done
  3.3 0.0 copy-done.1
  3.3 0.0 copy-done.2
  3.3 0.0 copy-done.3
  3.3 2.2 %shard_map.65 = (f32[4,128,512]{2,1,0:T(8,128)S(1)}, f32[32,24,128]{2,1,0:T(8,128)S(1)}, f32[2,16,128]{2,1,0:T(8,128)S(1)}, f32[4,8,128]{2,1,0:T(8,128)S(1)}) custom-call(f32[4,4,128,128]{3,2,1,0:T(8,128)S(1)} %copy-done, f32[4,4,128,128]{3,2,1,0:T(8,128)S(1)} %copy-done.1, f32[4,8,128]{2,1,0:T(8,128)S(1)} %get-tuple-element.29.hx, f32[4,4]{1,0:T(4,128)S(1)} %copy-done.2, ...), custom_call_target="tpu_custom_call" | custom-call | flops 3000000000 | bytes 3000000 | tf_op jit(solution)/shard_map/pallas_call | solution.py:442
  5.5 18.6 %all_to_all.20.recv = f32[32,24,128]{2,1,0:T(8,128)S(1)} all-to-all(f32[32,24,128]{2,1,0:T(8,128)S(1)} %get-tuple-element.33), channel_id=1, replica_groups=mesh['row'=32,'col'=8] {'row'}, dimensions={0} | all-to-all | bytes 786432 | tf_op jit(solution)/shard_map/all_to_all | solution.py:478
  24.1 1.3 %shard_map.66 = (f32[4,4,128,128]{3,2,1,0:T(8,128)S(1)}, f32[8,16,128]{2,1,0:T(8,128)S(1)}, f32[2,16,128]{2,1,0:T(8,128)S(1)}) custom-call(f32[4,128,512]{2,1,0:T(8,128)S(1)} %get-tuple-element.30.f_in, f32[2,16,128]{2,1,0:T(8,128)S(1)} %get-tuple-element.31.cells, f32[4,8,128]{2,1,0:T(8,128)S(1)} %get-tuple-element.32.cols, ...), custom_call_target="tpu_custom_call" | custom-call | flops 3000000000 | bytes 3000000 | tf_op jit(solution)/shard_map/pallas_call | solution.py:442
  25.4 15.2 %all_to_all.21.recv = f32[8,16,128]{2,1,0:T(8,128)S(1)} all-to-all(f32[8,16,128]{2,1,0:T(8,128)S(1)} %get-tuple-element.41), channel_id=1, replica_groups=mesh['row'=32,'col'=8] {'col'}, dimensions={0} | all-to-all | bytes 131072 | tf_op jit(solution)/shard_map/all_to_all | solution.py:482
  40.6 3.0 %shard_map.67 = (f32[4,128,512]{2,1,0:T(8,128)S(1)}, f32[32,24,128]{2,1,0:T(8,128)S(1)}, f32[2,16,128]{2,1,0:T(8,128)S(1)}, f32[4,8,128]{2,1,0:T(8,128)S(1)}) custom-call(f32[4,4,128,128]{3,2,1,0:T(8,128)S(1)} %get-tuple-element.40.g_in, f32[8,16,128]{2,1,0:T(8,128)S(1)} %all_to_all.21.recv, f32[2,16,128]{2,1,0:T(8,128)S(1)} %get-tuple-element.42.beside, ...), custom_call_target="tpu_custom_call" | custom-call | flops 3000000000 | bytes 3000000 | tf_op jit(solution)/shard_map/pallas_call | solution.py:442
  43.6 15.2 %all_to_all.22.recv = f32[32,24,128]{2,1,0:T(8,128)S(1)} all-to-all(f32[32,24,128]{2,1,0:T(8,128)S(1)} %get-tuple-element.49), channel_id=1, replica_groups=mesh['row'=32,'col'=8] {'row'}, dimensions={0} | all-to-all | bytes 786432 | tf_op jit(solution)/shard_map/all_to_all | solution.py:478
  58.7 1.3 %shard_map.68 = (f32[4,4,128,128]{3,2,1,0:T(8,128)S(1)}, f32[8,16,128]{2,1,0:T(8,128)S(1)}, f32[2,16,128]{2,1,0:T(8,128)S(1)}) custom-call(f32[4,128,512]{2,1,0:T(8,128)S(1)} %get-tuple-element.46.f_in, f32[2,16,128]{2,1,0:T(8,128)S(1)} %get-tuple-element.47.cells, f32[4,8,128]{2,1,0:T(8,128)S(1)} %get-tuple-element.48.cols, ...), custom_call_target="tpu_custom_call" | custom-call | flops 3000000000 | bytes 3000000 | tf_op jit(solution)/shard_map/pallas_call | solution.py:442
  60.1 9.5 %all_to_all.23.recv = f32[8,16,128]{2,1,0:T(8,128)S(1)} all-to-all(f32[8,16,128]{2,1,0:T(8,128)S(1)} %get-tuple-element.51), channel_id=1, replica_groups=mesh['row'=32,'col'=8] {'col'}, dimensions={0} | all-to-all | bytes 131072 | tf_op jit(solution)/shard_map/all_to_all | solution.py:482
  69.6 1.7 %shard_map.69 = f32[4,4,128,128]{3,2,1,0:T(8,128)} custom-call(f32[4,4,128,128]{3,2,1,0:T(8,128)S(1)} %get-tuple-element.50.g_in, f32[8,16,128]{2,1,0:T(8,128)S(1)} %all_to_all.23.recv, f32[2,16,128]{2,1,0:T(8,128)S(1)} %get-tuple-element.52.beside, f32[32,128]{1,0:T(8,128)S(1)} %get-tuple-element.43.wy, f32[4,128,128]{2,1,0:T(8,128)S(1)} %get-tuple-element.44.gy, ...), custom_call_target="tpu_custom_call" | custom-call | flops 3000000000 | bytes 3000000 | tf_op jit(solution)/shard_map/pallas_call | solution.py:442
Async XLA Ops:
  0.9 2.4 %copy-start = (f32[4,4,128,128]{3,2,1,0:T(8,128)S(1)}, f32[4,4,128,128]{3,2,1,0:T(8,128)}, u32[]{:S(2)}) copy-start(f32[4,4,128,128]{3,2,1,0:T(8,128)} %state.1) | copy-start | bytes 3145732
  0.9 2.4 %copy-start.1 = (f32[4,4,128,128]{3,2,1,0:T(8,128)S(1)}, f32[4,4,128,128]{3,2,1,0:T(8,128)}, u32[]{:S(2)}) copy-start(f32[4,4,128,128]{3,2,1,0:T(8,128)} %rate.3) | copy-start | bytes 3145732
  0.9 2.4 %copy-start.2 = (f32[4,4]{1,0:T(4,128)S(1)}, f32[4,4]{1,0:T(4,128)}, u32[]{:S(2)}) copy-start(f32[4,4]{1,0:T(4,128)} %kin.3) | copy-start | bytes 196
  0.9 2.4 %copy-start.3 = (f32[4,4]{1,0:T(4,128)S(1)}, f32[4,4]{1,0:T(4,128)}, u32[]{:S(2)}) copy-start(f32[4,4]{1,0:T(4,128)} %cross.3) | copy-start | bytes 196

commit v6 on v5

--- a/solution.py
+++ b/solution.py
@@ -250,6 +250,10 @@
             jnp.where(r8 == 1, qr * inv_q, jnp.where(r8 == 2, beside, 0.0)),
         )
 
+    wide = iota((N, 4 * N), 0)
+    line, plane = wide % 16, iota((N, 4 * N), 1) // N
+    from_after, high = (wide // 16) % 2 == 1, wide < 64
+
     for s in range(4):
         at = slice(32 + s, 33 + s)
         pr, qr, er = phi_t[at], psi_t[at], eps_t[at]
@@ -268,7 +272,14 @@
         ends = phi_before[:, at], phi_after[:, at], psi_before[:, at], psi_after[:, at]
         pb, pa, qb, qa = ends
         gy[s] = jnp.where(low, qc * (pr * er), pc * (qr * er))
-        ry[s] = jnp.where(r8 == 0, pb * qr * er, jnp.where(r8 == 1, qa * pr * er, 0.0))
+        lam, mu = split(pb * qr * er), split(qa * pr * er)
+        part = [
+            jnp.where(from_after, jnp.concatenate([m] * 4, 1), jnp.concatenate([v] * 4, 1))
+            for v, m in zip(lam, mu)
+        ]
+        ry[s] = jnp.where(
+            line == 4 * s + plane, jnp.where(high, part[0], part[1]), 0.0
+        ).astype(bf16)
         hy[s] = from_either_end(pr, qr, ends)
 
 
@@ -391,36 +402,28 @@
         send[m] = pay[(m < l).astype(jnp.int32)]
 
 
-def finish_cols(ny, g_in, recv, beside, wy, gy, ry, out, turned, done=None):
+def finish_cols(ny, g_in, recv, beside, wy, gy, ry, out, done=None):
     incoming = dot_mixed(wy[...], recv[...].reshape(ny * 16, N))
-    turned[...] = jnp.concatenate(
-        [
-            incoming[0:16] + beside[0],
-            incoming[16:32] + beside[1],
-            jnp.zeros((N - 32, N), f32),
-        ],
-        axis=0,
-    ).T
+    lines = split(
+        jnp.concatenate([incoming[0:16] + beside[0], incoming[16:32] + beside[1]], axis=0)
+    )
+    lines = jnp.concatenate(lines + lines, axis=0).T
     for s in range(4):
         res = dot_cols(g_in[s].reshape(4 * N, N), gy[s])
-        lam, mu = ry[s, 0:1], ry[s, 1:2]
+        outer = bdot(lines, ry[s])
         for z in range(4):
-            q = 4 * s + z
-            out[s, z] = (
-                res[z * N : (z + 1) * N]
-                + turned[:, q : q + 1] * lam
-                + turned[:, 16 + q : 17 + q] * mu
-            )
+            at = slice(z * N, (z + 1) * N)
+            out[s, z] = res[at] + outer[:, at]
         if done is not None:
             done(s)
 
 
-def last_kernel(ny, g_in, recv, beside, wy, gy, ry, out, state, turned, sent):
+def last_kernel(ny, g_in, recv, beside, wy, gy, ry, out, state, sent):
     copies = [
         pltpu.make_async_copy(state.at[s], out.at[s], sent.at[s]) for s in range(4)
     ]
     finish_cols(
-        ny, g_in, recv, beside, wy, gy, ry, state, turned, lambda s: copies[s].start()
+        ny, g_in, recv, beside, wy, gy, ry, state, lambda s: copies[s].start()
     )
     for copy in copies:
         copy.wait()
@@ -428,14 +431,17 @@
 
 def next_kernel(
     nx, ny, g_in, recv, beside, wy, gy, ry, rate, hx, kin, cross,
-    f_out, send, cells, cols, state, turned, pay,
+    f_out, send, cells, cols, state, pay,
 ):
-    finish_cols(ny, g_in, recv, beside, wy, gy, ry, state, turned)
+    finish_cols(ny, g_in, recv, beside, wy, gy, ry, state)
     explicit(nx, ny, state, rate, hx, kin, cross, f_out, send, cells, cols, pay)
 
 
 def call(body, outs, scratch, smem=0, place_out=pltpu.VMEM):
-    shapes = [jax.ShapeDtypeStruct(shape, f32) for shape in outs]
+    shapes = [
+        jax.ShapeDtypeStruct(shape, f32) if isinstance(shape, tuple) else shape
+        for shape in outs
+    ]
 
     def run(*args):
         count = len(args) - smem
@@ -461,10 +467,11 @@
 def on_device(adjoint, rate_scale, kinetics, cross_matrix, x_diffusion, y_diffusion):
     nx, ny = lax.axis_size("row"), lax.axis_size("col")
     part = functools.partial
+    weights = jax.ShapeDtypeStruct((4, N, 4 * N), bf16)
     gx, lx, rx, hx, gy, ry, hy, wx, wx_cols, wy = call(
         part(tables_kernel, nx, ny),
         [
-            (4, N, N), (4, N, N), (4, 8, N), (4, 8, N), (4, N, N), (4, 8, N), (4, 8, N),
+            (4, N, N), (4, N, N), (4, 8, N), (4, 8, N), (4, N, N), weights, (4, 8, N),
             (32, nx * 16), (2, nx, N), (32, ny * 16),
         ],
         [(N, N)] * 8,
@@ -482,12 +489,12 @@
         recv = lax.all_to_all(send, "col", 0, 0, tiled=True)
         if step + 1 < STEPS:
             f, send, cells, cols = call(
-                part(next_kernel, nx, ny), step_out, [tile, (N, N), (2, 24, N)], 2
+                part(next_kernel, nx, ny), step_out, [tile, (2, 24, N)], 2
             )(g, recv, beside, wy, gy, ry, rate_scale, hx, kinetics, cross_matrix)
     (out,) = call(
         part(last_kernel, ny),
         [tile],
-        [tile, (N, N), pltpu.SemaphoreType.DMA((4,))],
+        [tile, pltpu.SemaphoreType.DMA((4,))],
         place_out=pl.ANY,
     )(g, recv, beside, wy, gy, ry)
     return out

time: 71.6 us -> 71.2 us (level)
  no operation moved by 1% of the time
where the time goes in v6:
time: 71.2 us; the launch traced here: 70.8 us
  blocking collectives  58.5 us (82%)
  Pallas kernels  11.4 us (16%)
  other arithmetic  0.89 us (1%)
    all_to_all x2, blocking collectives, on_device(): recv = lax.all_to_all(send, 'row', 0, 0, tiled=True)  33.7 us
    all_to_all x2, blocking collectives, on_device(): recv = lax.all_to_all(send, 'col', 0, 0, tiled=True)  24.7 us
    pallas_call x6, Pallas kernels, run(): pl.pallas_call(body, out_shape=shapes, in_specs=[pl.BlockSpec(memory_spac...  11.4 us

profile of v6, /device:TPU:1, one launch (start us, length us, event | category | flops | bytes accessed | tf_op | source)
XLA Modules:
  0.0 70.8 jit_solution(15382945880444116034)
XLA Ops:
  0.0 0.9 %fusion.eps_all = f32[4,5120]{1,0:T(4,128)S(1)} fusion(f32[4,1024]{1,0:T(4,128)} %param.11, f32[4,4096]{1,0:T(4,128)} %param.10), kind=kLoop, calls=%fused_computation.1 | loop fusion | flops 61440 | bytes 163840 | tf_op jit(solution)/shard_map/div | solution.py:478
  0.9 0.0 copy-start
  0.9 0.0 copy-start.1
  0.9 0.0 copy-start.2
  0.9 0.0 copy-start.3
  0.9 2.4 %shard_map.64 = (f32[4,128,128]{2,1,0:T(8,128)S(1)}, f32[4,128,128]{2,1,0:T(8,128)S(1)}, f32[4,8,128]{2,1,0:T(8,128)S(1)}, f32[4,8,128]{2,1,0:T(8,128)S(1)}, f32...) custom-call(f32[4,5120]{1,0:T(4,128)S(1)} %fusion.eps_all), custom_call_target="tpu_custom_call" | custom-call | flops 3000000000 | bytes 3000000 | tf_op jit(solution)/shard_map/pallas_call | solution.py:448
  3.3 0.0 copy-done
  3.3 0.0 copy-done.1
  3.3 0.0 copy-done.2
  3.3 0.0 copy-done.3
  3.4 2.2 %shard_map.65 = (f32[4,128,512]{2,1,0:T(8,128)S(1)}, f32[32,24,128]{2,1,0:T(8,128)S(1)}, f32[2,16,128]{2,1,0:T(8,128)S(1)}, f32[4,8,128]{2,1,0:T(8,128)S(1)}) custom-call(f32[4,4,128,128]{3,2,1,0:T(8,128)S(1)} %copy-done, f32[4,4,128,128]{3,2,1,0:T(8,128)S(1)} %copy-done.1, f32[4,8,128]{2,1,0:T(8,128)S(1)} %get-tuple-element.29.hx, f32[4,4]{1,0:T(4,128)S(1)} %copy-done.2, ...), custom_call_target="tpu_custom_call" | custom-call | flops 3000000000 | bytes 3000000 | tf_op jit(solution)/shard_map/pallas_call | solution.py:448
  5.6 18.6 %all_to_all.20.recv = f32[32,24,128]{2,1,0:T(8,128)S(1)} all-to-all(f32[32,24,128]{2,1,0:T(8,128)S(1)} %get-tuple-element.33), channel_id=1, replica_groups=mesh['row'=32,'col'=8] {'row'}, dimensions={0} | all-to-all | bytes 786432 | tf_op jit(solution)/shard_map/all_to_all | solution.py:485
  24.1 1.3 %shard_map.66 = (f32[4,4,128,128]{3,2,1,0:T(8,128)S(1)}, f32[8,16,128]{2,1,0:T(8,128)S(1)}, f32[2,16,128]{2,1,0:T(8,128)S(1)}) custom-call(f32[4,128,512]{2,1,0:T(8,128)S(1)} %get-tuple-element.30.f_in, f32[2,16,128]{2,1,0:T(8,128)S(1)} %get-tuple-element.31.cells, f32[4,8,128]{2,1,0:T(8,128)S(1)} %get-tuple-element.32.cols, ...), custom_call_target="tpu_custom_call" | custom-call | flops 3000000000 | bytes 3000000 | tf_op jit(solution)/shard_map/pallas_call | solution.py:448
  25.4 15.2 %all_to_all.21.recv = f32[8,16,128]{2,1,0:T(8,128)S(1)} all-to-all(f32[8,16,128]{2,1,0:T(8,128)S(1)} %get-tuple-element.41), channel_id=1, replica_groups=mesh['row'=32,'col'=8] {'col'}, dimensions={0} | all-to-all | bytes 131072 | tf_op jit(solution)/shard_map/all_to_all | solution.py:489
  40.7 2.6 %shard_map.67 = (f32[4,128,512]{2,1,0:T(8,128)S(1)}, f32[32,24,128]{2,1,0:T(8,128)S(1)}, f32[2,16,128]{2,1,0:T(8,128)S(1)}, f32[4,8,128]{2,1,0:T(8,128)S(1)}) custom-call(f32[4,4,128,128]{3,2,1,0:T(8,128)S(1)} %get-tuple-element.40.g_in, f32[8,16,128]{2,1,0:T(8,128)S(1)} %all_to_all.21.recv, f32[2,16,128]{2,1,0:T(8,128)S(1)} %get-tuple-element.42.beside, ...), custom_call_target="tpu_custom_call" | custom-call | flops 3000000000 | bytes 3000000 | tf_op jit(solution)/shard_map/pallas_call | solution.py:448
  43.3 15.2 %all_to_all.22.recv = f32[32,24,128]{2,1,0:T(8,128)S(1)} all-to-all(f32[32,24,128]{2,1,0:T(8,128)S(1)} %get-tuple-element.49), channel_id=1, replica_groups=mesh['row'=32,'col'=8] {'row'}, dimensions={0} | all-to-all | bytes 786432 | tf_op jit(solution)/shard_map/all_to_all | solution.py:485
  58.5 1.3 %shard_map.68 = (f32[4,4,128,128]{3,2,1,0:T(8,128)S(1)}, f32[8,16,128]{2,1,0:T(8,128)S(1)}, f32[2,16,128]{2,1,0:T(8,128)S(1)}) custom-call(f32[4,128,512]{2,1,0:T(8,128)S(1)} %get-tuple-element.46.f_in, f32[2,16,128]{2,1,0:T(8,128)S(1)} %get-tuple-element.47.cells, f32[4,8,128]{2,1,0:T(8,128)S(1)} %get-tuple-element.48.cols, ...), custom_call_target="tpu_custom_call" | custom-call | flops 3000000000 | bytes 3000000 | tf_op jit(solution)/shard_map/pallas_call | solution.py:448
  59.8 9.5 %all_to_all.23.recv = f32[8,16,128]{2,1,0:T(8,128)S(1)} all-to-all(f32[8,16,128]{2,1,0:T(8,128)S(1)} %get-tuple-element.51), channel_id=1, replica_groups=mesh['row'=32,'col'=8] {'col'}, dimensions={0} | all-to-all | bytes 131072 | tf_op jit(solution)/shard_map/all_to_all | solution.py:489
  69.3 1.5 %shard_map.69 = f32[4,4,128,128]{3,2,1,0:T(8,128)} custom-call(f32[4,4,128,128]{3,2,1,0:T(8,128)S(1)} %get-tuple-element.50.g_in, f32[8,16,128]{2,1,0:T(8,128)S(1)} %all_to_all.23.recv, f32[2,16,128]{2,1,0:T(8,128)S(1)} %get-tuple-element.52.beside, f32[32,128]{1,0:T(8,128)S(1)} %get-tuple-element.43.wy, f32[4,128,128]{2,1,0:T(8,128)S(1)} %get-tuple-element.44.gy, ...), custom_call_target="tpu_custom_call" | custom-call | flops 3000000000 | bytes 3000000 | tf_op jit(solution)/shard_map/pallas_call | solution.py:448
Async XLA Ops:
  0.9 2.4 %copy-start = (f32[4,4,128,128]{3,2,1,0:T(8,128)S(1)}, f32[4,4,128,128]{3,2,1,0:T(8,128)}, u32[]{:S(2)}) copy-start(f32[4,4,128,128]{3,2,1,0:T(8,128)} %state.1) | copy-start | bytes 3145732
  0.9 2.4 %copy-start.1 = (f32[4,4,128,128]{3,2,1,0:T(8,128)S(1)}, f32[4,4,128,128]{3,2,1,0:T(8,128)}, u32[]{:S(2)}) copy-start(f32[4,4,128,128]{3,2,1,0:T(8,128)} %rate.3) | copy-start | bytes 3145732
  0.9 2.4 %copy-start.2 = (f32[4,4]{1,0:T(4,128)S(1)}, f32[4,4]{1,0:T(4,128)}, u32[]{:S(2)}) copy-start(f32[4,4]{1,0:T(4,128)} %kin.3) | copy-start | bytes 196
  0.9 2.4 %copy-start.3 = (f32[4,4]{1,0:T(4,128)S(1)}, f32[4,4]{1,0:T(4,128)}, u32[]{:S(2)}) copy-start(f32[4,4]{1,0:T(4,128)} %cross.3) | copy-start | bytes 196

commit v7 on v6

--- a/solution.py
+++ b/solution.py
@@ -71,7 +71,7 @@
 
 
 def tables_kernel(
-    nx, ny, eps_all, gx, lx, rx, hx, gy, ry, hy, wx, wx_cols, wy,
+    nx, ny, eps_all, gx, lx, rx, hx, gy, ry, hy, wx, wy,
     rows_x, rows_y, ex, ey, p0, p1, q0, q1,
 ):
     k = lax.axis_index("row")
@@ -194,18 +194,8 @@
         hit = (src // 4 == col // per_block) & (src % 4 == species_of(col % per_block))
         return pick(weight, hit)
 
-    width = nx * 16
-    spread = expand(width, 16, lambda r: r // 4)
-    rr, cc = iota((32, width), 0), iota((32, width), 1)
-    wx[...] = jnp.where(
-        rr % 16 == cc % 16, jnp.where(rr < 16, spread[0:1], spread[2:3]), 0.0
-    )
-    own_lanes = iota((nx, N), 1) // 4 == iota((nx, N), 0)
-    by_species = iota((N, N), 0) % 4 == iota((N, N), 1)
-    for p in range(2):
-        wx_cols[p] = pick(
-            jnp.where(own_lanes, weight[2 * p : 2 * p + 1], 0.0), by_species
-        )
+    both = jnp.where(row < 4, weight[0:1], weight[2:3])
+    wx[...] = jnp.where(lane % 4 == row % 4, both, 0.0)[:, 0 : nx * 4]
     width = ny * 16
     spread = expand(width, 16, lambda r: r // 4)
     rr, cc = iota((32, width), 0), iota((32, width), 1)
@@ -327,10 +317,10 @@
             q = 4 * s + z
             side = jnp.where(j0 // 2 == q, pltpu.roll(state[s, z], 2 * q + 1, 1), side)
     side = side.T
-    r8, c8 = iota((8, N), 0), iota((8, N), 1)
+    r8 = iota((8, N), 0)
     has = 0.25 * jnp.where(r8 % 2 == 0, (l < ny - 1).astype(f32), (l > 0).astype(f32))
     has_x = 0.25 * (k > 0).astype(f32), 0.25 * (k < nx - 1).astype(f32)
-    tails = [jnp.zeros((8, N), f32)] * 2
+    pay[...] = jnp.zeros_like(pay)
     for j in range(4):
         mix = cross[0, j] * side[0:8]
         for i in range(1, 4):
@@ -346,45 +336,42 @@
                     piece = piece + cross[i, j] * state[i, z, row : row + 1, :]
                 pieces.append(has_x[p] * piece)
             beside.append(jnp.concatenate(pieces, axis=1))
-            by_plane(cells, p, j, beside[p])
+            cells[p, j : j + 1, :] = beside[p]
         sums = dot_rows(hx[j], f_out[j])
+        ends = dot_rows(hx[j], mix, nt=True)
         for p in range(2):
             c = hx[j, 2:3, 2 * p : 2 * p + 1], hx[j, 2:3, 2 * p + 1 : 2 * p + 2]
-            by_plane(pay, p, j, sums[p : p + 1] + c[0] * beside[0] + c[1] * beside[1])
-            total = jnp.sum(mix * hx[j, p : p + 1, :], axis=1, keepdims=True)
-            tails[p] = jnp.where(c8 == j, total, tails[p])
-    for p in range(2):
-        pay[p, 16:24, :] = tails[p]
+            pay[p, j : j + 1, 0 : 4 * N] = (
+                sums[p : p + 1] + c[0] * beside[0] + c[1] * beside[1]
+            )
+            pay[p, j : j + 1, 4 * N : 4 * N + 8] = ends[p : p + 1]
     for j in range(nx):
         send[j] = pay[(j < k).astype(jnp.int32)]
 
 
 def rows_kernel(
-    nx, ny, f_in, cells, cols, recv, wx, wx_cols, gx, lx, rx, hy, g_out, send, beside, pay
+    nx, ny, f_in, cells, cols, recv, wx, gx, lx, rx, hy, g_out, send, beside, pay
 ):
     l = lax.axis_index("col")
-    incoming = dot_mixed(wx[...], recv[:, 0:16, :].reshape(nx * 16, N))
-    from_before = incoming[0:16] + cells[0]
-    from_after = incoming[16:32] + cells[1]
-    in_cols = []
-    for p in range(2):
-        total = recv[0, 16:24, :] * wx_cols[p, 0:1, :]
-        for j in range(1, nx):
-            total = total + recv[j, 16:24, :] * wx_cols[p, j : j + 1, :]
-        in_cols.append(total)
+    incoming = dot_rows(wx[...], recv[...].reshape(nx * 4, 5 * N))
+    from_before = incoming[0:4, 0 : 4 * N] + cells[0]
+    from_after = incoming[4:8, 0 : 4 * N] + cells[1]
+    in_cols = jnp.concatenate(
+        [incoming[:, 4 * N :], jnp.zeros((N - 8, N), f32)], axis=0
+    ).T
     for s in range(4):
         g = dot_rows(gx[s], f_in[s])
         lam, mu = lx[s, :, 0:1], lx[s, :, 1:2]
         col = (
             dot_rows(cols[s], gx[s], nt=True)
-            + in_cols[0][:, s : s + 1] * rx[s, 0:1]
-            + in_cols[1][:, s : s + 1] * rx[s, 1:2]
+            + in_cols[0:8, s : s + 1] * rx[s, 0:1]
+            + in_cols[0:8, 4 + s : 5 + s] * rx[s, 1:2]
         )
         parts = []
         for z in range(4):
-            q = slice(4 * s + z, 4 * s + z + 1)
+            at = slice(z * N, (z + 1) * N)
             part = (
-                g[:, z * N : (z + 1) * N] + lam * from_before[q] + mu * from_after[q]
+                g[:, at] + lam * from_before[s : s + 1, at] + mu * from_after[s : s + 1, at]
             )
             g_out[s, z] = part
             parts.append(part)
@@ -468,28 +455,28 @@
     nx, ny = lax.axis_size("row"), lax.axis_size("col")
     part = functools.partial
     weights = jax.ShapeDtypeStruct((4, N, 4 * N), bf16)
-    gx, lx, rx, hx, gy, ry, hy, wx, wx_cols, wy = call(
+    gx, lx, rx, hx, gy, ry, hy, wx, wy = call(
         part(tables_kernel, nx, ny),
         [
             (4, N, N), (4, N, N), (4, 8, N), (4, 8, N), (4, N, N), weights, (4, 8, N),
-            (32, nx * 16), (2, nx, N), (32, ny * 16),
+            (8, nx * 4), (32, ny * 16),
         ],
         [(N, N)] * 8,
     )(1.0 / (M * jnp.concatenate([x_diffusion, y_diffusion], axis=1)))
     tile = (4, 4, N, N)
-    step_out = [(4, N, 4 * N), (nx, 24, N), (2, 16, N), (4, 8, N)]
-    f, send, cells, cols = call(part(explicit, nx, ny), step_out, [(2, 24, N)], 2)(
+    step_out = [(4, N, 4 * N), (nx, 4, 5 * N), (2, 4, 4 * N), (4, 8, N)]
+    f, send, cells, cols = call(part(explicit, nx, ny), step_out, [(2, 4, 5 * N)], 2)(
         adjoint, rate_scale, hx, kinetics, cross_matrix
     )
     for step in range(STEPS):
         recv = lax.all_to_all(send, "row", 0, 0, tiled=True)
         g, send, beside = call(
             part(rows_kernel, nx, ny), [tile, (ny, 16, N), (2, 16, N)], [(2, 16, N)]
-        )(f, cells, cols, recv, wx, wx_cols, gx, lx, rx, hy)
+        )(f, cells, cols, recv, wx, gx, lx, rx, hy)
         recv = lax.all_to_all(send, "col", 0, 0, tiled=True)
         if step + 1 < STEPS:
             f, send, cells, cols = call(
-                part(next_kernel, nx, ny), step_out, [tile, (2, 24, N)], 2
+                part(next_kernel, nx, ny), step_out, [tile, (2, 4, 5 * N)], 2
             )(g, recv, beside, wy, gy, ry, rate_scale, hx, kinetics, cross_matrix)
     (out,) = call(
         part(last_kernel, ny),

time: 71.2 us -> 69.7 us (0.979)
  blocking collectives: 58.5 us -> 57.2 us
    all_to_all x2, blocking collectives: 33.7 us -> 32.4 us  [on_device(): recv = lax.all_to_all(send, 'row', 0, 0, tiled=True)]
where the time goes in v7:
time: 69.7 us; the launch traced here: 69.3 us
  blocking collectives  57.2 us (82%)
  Pallas kernels  11.2 us (16%)
  other arithmetic  0.89 us (1%)
    all_to_all x2, blocking collectives, on_device(): recv = lax.all_to_all(send, 'row', 0, 0, tiled=True)  32.4 us
    all_to_all x2, blocking collectives, on_device(): recv = lax.all_to_all(send, 'col', 0, 0, tiled=True)  24.7 us
    pallas_call x6, Pallas kernels, run(): pl.pallas_call(body, out_shape=shapes, in_specs=[pl.BlockSpec(memory_spac...  11.2 us

profile of v7, /device:TPU:1, one launch (start us, length us, event | category | flops | bytes accessed | tf_op | source)
XLA Modules:
  0.0 69.3 jit_solution(5545258623840039242)
XLA Ops:
  0.0 0.9 %fusion.eps_all = f32[4,5120]{1,0:T(4,128)S(1)} fusion(f32[4,1024]{1,0:T(4,128)} %param.11, f32[4,4096]{1,0:T(4,128)} %param.10), kind=kLoop, calls=%fused_computation.1 | loop fusion | flops 61440 | bytes 163840 | tf_op jit(solution)/shard_map/div | solution.py:465
  0.9 0.0 copy-start
  0.9 0.0 copy-start.1
  0.9 0.0 copy-start.2
  0.9 0.0 copy-start.3
  0.9 2.2 %shard_map.64 = (f32[4,128,128]{2,1,0:T(8,128)S(1)}, f32[4,128,128]{2,1,0:T(8,128)S(1)}, f32[4,8,128]{2,1,0:T(8,128)S(1)}, f32[4,8,128]{2,1,0:T(8,128)S(1)}, f32...) custom-call(f32[4,5120]{1,0:T(4,128)S(1)} %fusion.eps_all), custom_call_target="tpu_custom_call" | custom-call | flops 3000000000 | bytes 3000000 | tf_op jit(solution)/shard_map/pallas_call | solution.py:435
  3.2 0.0 copy-done
  3.2 0.0 copy-done.1
  3.2 0.0 copy-done.2
  3.2 0.0 copy-done.3
  3.2 2.2 %shard_map.65 = (f32[4,128,512]{2,1,0:T(8,128)S(1)}, f32[32,4,640]{2,1,0:T(4,128)S(1)}, f32[2,4,512]{2,1,0:T(4,128)S(1)}, f32[4,8,128]{2,1,0:T(8,128)S(1)}) custom-call(f32[4,4,128,128]{3,2,1,0:T(8,128)S(1)} %copy-done, f32[4,4,128,128]{3,2,1,0:T(8,128)S(1)} %copy-done.1, f32[4,8,128]{2,1,0:T(8,128)S(1)} %get-tuple-element.28.hx, f32[4,4]{1,0:T(4,128)S(1)} %copy-done.2, ...), custom_call_target="tpu_custom_call" | custom-call | flops 3000000000 | bytes 3000000 | tf_op jit(solution)/shard_map/pallas_call | solution.py:435
  5.4 17.9 %all_to_all.20.recv = f32[32,4,640]{2,1,0:T(4,128)S(1)} all-to-all(f32[32,4,640]{2,1,0:T(4,128)S(1)} %get-tuple-element.32), channel_id=1, replica_groups=mesh['row'=32,'col'=8] {'row'}, dimensions={0} | all-to-all | bytes 655360 | tf_op jit(solution)/shard_map/all_to_all | solution.py:472
  23.4 1.3 %shard_map.66 = (f32[4,4,128,128]{3,2,1,0:T(8,128)S(1)}, f32[8,16,128]{2,1,0:T(8,128)S(1)}, f32[2,16,128]{2,1,0:T(8,128)S(1)}) custom-call(f32[4,128,512]{2,1,0:T(8,128)S(1)} %get-tuple-element.29.f_in, f32[2,4,512]{2,1,0:T(4,128)S(1)} %get-tuple-element.30.cells, f32[4,8,128]{2,1,0:T(8,128)S(1)} %get-tuple-element.31.cols, ...), custom_call_target="tpu_custom_call" | custom-call | flops 3000000000 | bytes 3000000 | tf_op jit(solution)/shard_map/pallas_call | solution.py:435
  24.7 15.2 %all_to_all.21.recv = f32[8,16,128]{2,1,0:T(8,128)S(1)} all-to-all(f32[8,16,128]{2,1,0:T(8,128)S(1)} %get-tuple-element.39), channel_id=1, replica_groups=mesh['row'=32,'col'=8] {'col'}, dimensions={0} | all-to-all | bytes 131072 | tf_op jit(solution)/shard_map/all_to_all | solution.py:476
  39.9 2.6 %shard_map.67 = (f32[4,128,512]{2,1,0:T(8,128)S(1)}, f32[32,4,640]{2,1,0:T(4,128)S(1)}, f32[2,4,512]{2,1,0:T(4,128)S(1)}, f32[4,8,128]{2,1,0:T(8,128)S(1)}) custom-call(f32[4,4,128,128]{3,2,1,0:T(8,128)S(1)} %get-tuple-element.38.g_in, f32[8,16,128]{2,1,0:T(8,128)S(1)} %all_to_all.21.recv, f32[2,16,128]{2,1,0:T(8,128)S(1)} %get-tuple-element.40.beside, ...), custom_call_target="tpu_custom_call" | custom-call | flops 3000000000 | bytes 3000000 | tf_op jit(solution)/shard_map/pallas_call | solution.py:435
  42.5 14.5 %all_to_all.22.recv = f32[32,4,640]{2,1,0:T(4,128)S(1)} all-to-all(f32[32,4,640]{2,1,0:T(4,128)S(1)} %get-tuple-element.47), channel_id=1, replica_groups=mesh['row'=32,'col'=8] {'row'}, dimensions={0} | all-to-all | bytes 655360 | tf_op jit(solution)/shard_map/all_to_all | solution.py:472
  57.0 1.3 %shard_map.68 = (f32[4,4,128,128]{3,2,1,0:T(8,128)S(1)}, f32[8,16,128]{2,1,0:T(8,128)S(1)}, f32[2,16,128]{2,1,0:T(8,128)S(1)}) custom-call(f32[4,128,512]{2,1,0:T(8,128)S(1)} %get-tuple-element.44.f_in, f32[2,4,512]{2,1,0:T(4,128)S(1)} %get-tuple-element.45.cells, f32[4,8,128]{2,1,0:T(8,128)S(1)} %get-tuple-element.46.cols, ...), custom_call_target="tpu_custom_call" | custom-call | flops 3000000000 | bytes 3000000 | tf_op jit(solution)/shard_map/pallas_call | solution.py:435
  58.3 9.5 %all_to_all.23.recv = f32[8,16,128]{2,1,0:T(8,128)S(1)} all-to-all(f32[8,16,128]{2,1,0:T(8,128)S(1)} %get-tuple-element.49), channel_id=1, replica_groups=mesh['row'=32,'col'=8] {'col'}, dimensions={0} | all-to-all | bytes 131072 | tf_op jit(solution)/shard_map/all_to_all | solution.py:476
  67.8 1.5 %shard_map.69 = f32[4,4,128,128]{3,2,1,0:T(8,128)} custom-call(f32[4,4,128,128]{3,2,1,0:T(8,128)S(1)} %get-tuple-element.48.g_in, f32[8,16,128]{2,1,0:T(8,128)S(1)} %all_to_all.23.recv, f32[2,16,128]{2,1,0:T(8,128)S(1)} %get-tuple-element.50.beside, f32[32,128]{1,0:T(8,128)S(1)} %get-tuple-element.41.wy, f32[4,128,128]{2,1,0:T(8,128)S(1)} %get-tuple-element.42.gy, ...), custom_call_target="tpu_custom_call" | custom-call | flops 3000000000 | bytes 3000000 | tf_op jit(solution)/shard_map/pallas_call | solution.py:435
Async XLA Ops:
  0.9 2.3 %copy-start = (f32[4,4,128,128]{3,2,1,0:T(8,128)S(1)}, f32[4,4,128,128]{3,2,1,0:T(8,128)}, u32[]{:S(2)}) copy-start(f32[4,4,128,128]{3,2,1,0:T(8,128)} %state.1) | copy-start | bytes 3145732
  0.9 2.3 %copy-start.1 = (f32[4,4,128,128]{3,2,1,0:T(8,128)S(1)}, f32[4,4,128,128]{3,2,1,0:T(8,128)}, u32[]{:S(2)}) copy-start(f32[4,4,128,128]{3,2,1,0:T(8,128)} %rate.3) | copy-start | bytes 3145732
  0.9 2.3 %copy-start.2 = (f32[4,4]{1,0:T(4,128)S(1)}, f32[4,4]{1,0:T(4,128)}, u32[]{:S(2)}) copy-start(f32[4,4]{1,0:T(4,128)} %kin.3) | copy-start | bytes 196
  0.9 2.3 %copy-start.3 = (f32[4,4]{1,0:T(4,128)S(1)}, f32[4,4]{1,0:T(4,128)}, u32[]{:S(2)}) copy-start(f32[4,4]{1,0:T(4,128)} %cross.3) | copy-start | bytes 196
